TPU v7x, 128 devices: a whole 4x4x4 slice. The times are simulated.
128 devices in a mesh: dp: 16 (over x_lo, z, core), tensor: 8 (over x_hi, y).
Axes of the slice: x: 4 (x_hi: 2, x_lo: 2; x = x_hi * 2 + x_lo), y: 4, z: 4, core: 2. Of those that a mesh axis runs over, the one named last changes fastest.
Arguments:
- tokens: bfloat16 [16384, 1024], P(('dp', 'tensor')), may hold values from -6 to 6
- lengths: int32 [16, 4], P('dp'), may hold values from 1 to 976, as said below
- w_qkv: bfloat16 [2, 1024, 3, 1024], P(None, 'dp', None, 'tensor'), may hold values from -0.1875 to 0.1875
- b_qv: bfloat16 [2, 2, 1024], replicated, may hold values from -3 to 3
- w_out: bfloat16 [2, 1024, 1024], P(None, 'tensor', 'dp'), may hold values from -0.5 to 0.5
- b_out: bfloat16 [2, 1024], replicated, may hold values from -3 to 3
- w_in: bfloat16 [2, 1024, 4096], P(None, 'dp', 'tensor'), may hold values from -0.1875 to 0.1875
- b_in: bfloat16 [2, 4096], replicated, may hold values from -3 to 3
- w_down: bfloat16 [2, 4096, 1024], P(None, 'tensor', 'dp'), may hold values from -0.09375 to 0.09375
- b_down: bfloat16 [2, 1024], replicated, may hold values from -3 to 3
- ln_gain: bfloat16 [2, 2, 1024], replicated, may hold values from 0.5 to 1.5
- ln_bias: bfloat16 [2, 2, 1024], replicated, may hold values from -2 to 2
- cotangent: bfloat16 [16384, 1024], P(('dp', 'tensor')), may hold values from -6 to 6
Outputs:
- encoded: bfloat16 [16384, 1024], P(('dp', 'tensor'))
- g_tokens: bfloat16 [16384, 1024], P(('dp', 'tensor'))
- g_w_qkv: float32 [2, 1024, 3, 1024], P(None, 'dp', None, 'tensor')
- g_b_qv: float32 [2, 2, 1024], replicated
- g_w_out: float32 [2, 1024, 1024], P(None, 'tensor', 'dp')
- g_b_out: float32 [2, 1024], replicated
- g_w_in: float32 [2, 1024, 4096], P(None, 'dp', 'tensor')
- g_b_in: float32 [2, 4096], replicated
- g_w_down: float32 [2, 4096, 1024], P(None, 'tensor', 'dp')
- g_b_down: float32 [2, 1024], replicated
- g_ln_gain: float32 [2, 2, 1024], replicated
- g_ln_bias: float32 [2, 2, 1024], replicated
Inputs may be any that keep to these rules, and one draw needn't show every extreme that they name: In each data shard exactly one sequence, at a place drawn from the seed, is long: between 897 and 976 tokens, with exactly 976 in some shard; the others have at most 16 tokens each. A shard's lengths sum to at most 1024.
All inputs are finite; a program needn't handle non-finite values.
Results may differ from a plain program's by a relative error of at most 0.028.
Values may be sent and summed in bfloat16 or wider, within the bound.
A program may use at most 128 MiB of HBM per device.

v0:
```python
import jax
import jax.numpy as jnp
from jax import lax
from jax.sharding import PartitionSpec as P

DH = 64


EPSILON = 1e-06


def layer_norm(stream, gain_vec, bias_vec):
    row_mean = jnp.mean(stream, axis=-1, keepdims=True)
    centered = stream - row_mean
    row_var = jnp.mean(centered * centered, axis=-1, keepdims=True)
    return centered * lax.rsqrt(row_var + EPSILON) * gain_vec + bias_vec


def exact_gelu(values):
    return jax.nn.gelu(values, approximate=False)


def segment_ids(shard_lengths, total_rows, seq_count):
    seq_ends = jnp.cumsum(shard_lengths)
    positions = jnp.arange(total_rows, dtype=jnp.int32)
    segments = jnp.sum((positions[:, None] >= seq_ends[None, :]).astype(jnp.int32), axis=1)
    return jnp.where(segments == seq_count, seq_count + positions, segments)


def masked_scores(queries, keys_in, allowed, score_scale):
    scores = (
        jnp.einsum("qhd,khd->hqk", queries, keys_in, preferred_element_type=jnp.float32)
        * score_scale
    )
    return jnp.where(allowed[None], scores, -1e30)


def attend_forward(queries, keys_in, values_in, allowed, score_scale):
    scores = masked_scores(queries, keys_in, allowed, score_scale)
    row_peak = jnp.max(scores, axis=-1, keepdims=True)
    exp_scores = jnp.exp(scores - row_peak)
    row_total = jnp.sum(exp_scores, axis=-1, keepdims=True)
    attn_probs = (exp_scores / row_total).astype(jnp.bfloat16)
    context = jnp.einsum("hqk,khd->qhd", attn_probs, values_in, preferred_element_type=jnp.float32)
    return (context, row_peak + jnp.log(row_total))


def attend_backward(queries, keys_in, values_in, allowed, score_scale, log_total, grad_context):
    scores = masked_scores(queries, keys_in, allowed, score_scale)
    attn_probs = jnp.exp(scores - log_total)
    probs_low = attn_probs.astype(jnp.bfloat16)
    grad_probs = jnp.einsum(
        "qhd,khd->hqk", grad_context, values_in, preferred_element_type=jnp.float32
    )
    grad_values = jnp.einsum(
        "hqk,qhd->khd", probs_low, grad_context, preferred_element_type=jnp.float32
    )
    row_inner = jnp.sum(attn_probs * grad_probs, axis=-1, keepdims=True)
    grad_scores = (attn_probs * (grad_probs - row_inner)).astype(jnp.bfloat16)
    grad_queries = (
        jnp.einsum("hqk,khd->qhd", grad_scores, keys_in, preferred_element_type=jnp.float32)
        * score_scale
    )
    grad_keys = (
        jnp.einsum("hqk,qhd->khd", grad_scores, queries, preferred_element_type=jnp.float32)
        * score_scale
    )
    return (grad_queries, grad_keys, grad_values)


def shards(
    tokens,
    lengths,
    w_qkv,
    b_qv,
    w_out,
    b_out,
    w_in,
    b_in,
    w_down,
    b_down,
    ln_gain,
    ln_bias,
    cotangent,
):
    groups = lax.axis_size("tensor")
    tensor_place = lax.axis_index("tensor")
    own_rows = tokens.shape[0]
    total_rows = own_rows * groups
    col_width = w_qkv.shape[3]
    hidden_width = w_in.shape[2]
    head_count = col_width // DH
    layers = w_qkv.shape[0]
    score_scale = DH ** (-0.5)
    segments = segment_ids(lengths[0], total_rows, lengths.shape[1])
    allowed = segments[:, None] == segments[None, :]
    contract_last = (((1,), (1,)), ((), ()))
    contract_first = (((0,), (0,)), ((), ()))

    def gather_rows(values):
        return lax.all_gather(values, "tensor", axis=0, tiled=True)

    def gather_grads(values):
        return lax.all_gather(values, "tensor", axis=0, tiled=True)

    def scatter_forward(values, weight):

        def term_rows(row_start, row_count):
            return jnp.dot(values, weight, preferred_element_type=jnp.float32)

        return lax.psum_scatter(
            term_rows(jnp.int32(0), own_rows * lax.axis_size("tensor")).astype(jnp.bfloat16),
            "tensor",
            scatter_dimension=0,
            tiled=True,
        ).astype(jnp.float32)

    def scatter_backward(values, weight):

        def term_rows(row_start, row_count):
            return lax.dot_general(
                values, weight, contract_last, preferred_element_type=jnp.float32
            )

        return lax.psum_scatter(
            term_rows(jnp.int32(0), own_rows * lax.axis_size("tensor")).astype(jnp.bfloat16),
            "tensor",
            scatter_dimension=0,
            tiled=True,
        ).astype(jnp.float32)

    def norm_params(layer_at, which):
        return (
            ln_gain[layer_at, which].astype(jnp.float32),
            ln_bias[layer_at, which].astype(jnp.float32),
        )

    hidden = tokens.astype(jnp.float32)
    stored_list = []
    for layer_at in range(layers):
        weights = (
            lax.all_gather(w_qkv[layer_at], "dp", axis=0, tiled=True),
            lax.all_gather(w_out[layer_at], "dp", axis=1, tiled=True),
            lax.all_gather(w_in[layer_at], "dp", axis=0, tiled=True),
            lax.all_gather(w_down[layer_at], "dp", axis=1, tiled=True),
        )
        layer_full_qkv, layer_full_out, layer_full_in, layer_full_down = weights
        layer_attn_input = gather_rows(hidden.astype(jnp.bfloat16))
        bias_qv = lax.dynamic_slice_in_dim(
            b_qv[layer_at].astype(jnp.float32), tensor_place * col_width, col_width, 1
        )
        bias_all = jnp.stack([bias_qv[0], jnp.zeros_like(bias_qv[0]), bias_qv[1]])
        qkv = jnp.einsum(
            "rd,dcj->rcj", layer_attn_input, layer_full_qkv, preferred_element_type=jnp.float32
        )
        layer_qkv_low = (qkv + bias_all).astype(jnp.bfloat16)
        layer_head_view = layer_qkv_low.reshape(total_rows, 3, head_count, DH)
        context, layer_log_total = attend_forward(
            layer_head_view[:, 0],
            layer_head_view[:, 1],
            layer_head_view[:, 2],
            allowed,
            score_scale,
        )
        layer_context_low = context.reshape(total_rows, col_width).astype(jnp.bfloat16)
        layer_first_sum = (
            hidden
            + scatter_forward(layer_context_low, layer_full_out)
            + b_out[layer_at].astype(jnp.float32)
        )
        layer_gain_one, layer_shift_one = norm_params(layer_at, 0)
        normed = layer_norm(layer_first_sum, layer_gain_one, layer_shift_one)
        layer_mlp_input = gather_rows(normed.astype(jnp.bfloat16))
        bias_in = lax.dynamic_slice_in_dim(
            b_in[layer_at].astype(jnp.float32), tensor_place * hidden_width, hidden_width, 0
        )
        layer_pre_gelu = (
            jnp.dot(layer_mlp_input, layer_full_in, preferred_element_type=jnp.float32) + bias_in
        )
        layer_act_low = exact_gelu(layer_pre_gelu).astype(jnp.bfloat16)
        layer_second_sum = (
            normed
            + scatter_forward(layer_act_low, layer_full_down)
            + b_down[layer_at].astype(jnp.float32)
        )
        layer_gain_two, layer_shift_two = norm_params(layer_at, 1)
        result = layer_norm(layer_second_sum, layer_gain_two, layer_shift_two)
        layer_stored = (
            hidden,
            layer_attn_input,
            layer_qkv_low,
            layer_log_total,
            layer_context_low,
            layer_first_sum,
            layer_mlp_input,
            layer_pre_gelu,
            layer_act_low,
            layer_second_sum,
            weights,
        )
        hidden = result
        stored = layer_stored
        stored_list.append(stored)
    encoded = hidden.astype(jnp.bfloat16)
    grad_hidden = cotangent.astype(jnp.float32)
    weight_list = []
    small_list = []
    for layer_at in reversed(range(layers)):
        stored = stored_list[layer_at]
        grad_out = grad_hidden
        (
            layer_hidden,
            attn_input,
            qkv_low,
            log_total,
            context_low,
            first_sum,
            mlp_input,
            pre_gelu,
            act_low,
            second_sum,
            layer_weights,
        ) = stored
        full_qkv, full_out, full_in, full_down = layer_weights
        gain_one, shift_one = norm_params(layer_at, 0)
        gain_two, shift_two = norm_params(layer_at, 1)
        second_pull = jax.vjp(layer_norm, second_sum, gain_two, shift_two)[1]
        grad_second, grad_gain_two, grad_shift_two = second_pull(grad_out)
        down_low = grad_second.astype(jnp.bfloat16)
        down_full = gather_grads(down_low)
        grad_act = lax.dot_general(
            down_full, full_down, contract_last, preferred_element_type=jnp.float32
        )
        grad_w_down = lax.dot_general(
            act_low, down_full, contract_first, preferred_element_type=jnp.float32
        )
        gelu_pull = jax.vjp(exact_gelu, pre_gelu)[1]
        pre_low = gelu_pull(grad_act)[0].astype(jnp.bfloat16)
        grad_w_in = lax.dot_general(
            mlp_input, pre_low, contract_first, preferred_element_type=jnp.float32
        )
        grad_normed = grad_second + scatter_backward(pre_low, full_in)
        first_pull = jax.vjp(layer_norm, first_sum, gain_one, shift_one)[1]
        grad_first, grad_gain_one, grad_shift_one = first_pull(grad_normed)
        attn_low = grad_first.astype(jnp.bfloat16)
        attn_full = gather_grads(attn_low)
        grad_context = lax.dot_general(
            attn_full, full_out, contract_last, preferred_element_type=jnp.float32
        )
        grad_context_low = grad_context.astype(jnp.bfloat16).reshape(total_rows, head_count, DH)
        grad_w_out = lax.dot_general(
            context_low, attn_full, contract_first, preferred_element_type=jnp.float32
        )
        head_view = qkv_low.reshape(total_rows, 3, head_count, DH)
        grad_queries, grad_keys, grad_values = attend_backward(
            head_view[:, 0],
            head_view[:, 1],
            head_view[:, 2],
            allowed,
            score_scale,
            log_total,
            grad_context_low,
        )
        grad_qkv_low = (
            jnp.stack([grad_queries, grad_keys, grad_values], axis=1)
            .reshape(total_rows, 3, col_width)
            .astype(jnp.bfloat16)
        )
        grad_w_qkv = jnp.einsum(
            "rd,rcj->dcj", attn_input, grad_qkv_low, preferred_element_type=jnp.float32
        )
        layer_grad_hidden = grad_first + scatter_backward(
            grad_qkv_low.reshape(total_rows, 3 * col_width),
            full_qkv.reshape(full_qkv.shape[0], 3 * col_width),
        )
        qkv_sums = jnp.sum(grad_qkv_low.astype(jnp.float32), axis=0)
        bias_qv_part = jnp.stack([qkv_sums[0], qkv_sums[2]])
        bias_qv_full = lax.dynamic_update_slice_in_dim(
            jnp.zeros((2, b_qv.shape[2]), jnp.float32), bias_qv_part, tensor_place * col_width, 1
        )
        bias_in_part = jnp.sum(pre_low.astype(jnp.float32), axis=0)
        bias_in_full = lax.dynamic_update_slice_in_dim(
            jnp.zeros((b_in.shape[1],), jnp.float32), bias_in_part, tensor_place * hidden_width, 0
        )
        bias_out_grad = jnp.sum(attn_low.astype(jnp.float32), axis=0)
        bias_down_grad = jnp.sum(down_low.astype(jnp.float32), axis=0)
        gain_grads = jnp.stack([grad_gain_one, grad_gain_two])
        shift_grads = jnp.stack([grad_shift_one, grad_shift_two])
        smalls = (
            bias_qv_full,
            bias_out_grad,
            bias_in_full,
            bias_down_grad,
            gain_grads,
            shift_grads,
        )
        grad_hidden, weight_grads, smalls = (
            layer_grad_hidden,
            (grad_w_qkv, grad_w_out, grad_w_in, grad_w_down),
            smalls,
        )
        weight_list.insert(0, weight_grads)
        small_list.insert(0, smalls)
    stacked = tuple(
        (jnp.stack([entry[position] for entry in weight_list]) for position in range(4))
    )
    stacked = (
        lax.psum_scatter(
            stacked[0].astype(jnp.bfloat16), "dp", scatter_dimension=1, tiled=True
        ).astype(jnp.float32),
        lax.psum_scatter(
            stacked[1].astype(jnp.bfloat16), "dp", scatter_dimension=2, tiled=True
        ).astype(jnp.float32),
        lax.psum_scatter(
            stacked[2].astype(jnp.bfloat16), "dp", scatter_dimension=1, tiled=True
        ).astype(jnp.float32),
        lax.psum_scatter(
            stacked[3].astype(jnp.bfloat16), "dp", scatter_dimension=2, tiled=True
        ).astype(jnp.float32),
    )
    small_stacked = tuple(
        (jnp.stack([entry[position] for entry in small_list]) for position in range(6))
    )
    small_sums = lax.psum(
        (
            small_stacked[0],
            small_stacked[1],
            small_stacked[2],
            small_stacked[3],
            small_stacked[4],
            small_stacked[5],
        ),
        ("dp", "tensor"),
    )
    g_tokens = grad_hidden.astype(jnp.bfloat16)
    return (
        encoded,
        g_tokens,
        stacked[0],
        small_sums[0],
        stacked[1],
        small_sums[1],
        stacked[2],
        small_sums[2],
        stacked[3],
        small_sums[3],
        small_sums[4],
        small_sums[5],
    )


def solution(mesh):
    placed = (
        P(("dp", "tensor"), None),
        P("dp", None),
        P(None, "dp", None, "tensor"),
        P(),
        P(None, "tensor", "dp"),
        P(),
        P(None, "dp", "tensor"),
        P(),
        P(None, "tensor", "dp"),
        P(),
        P(),
        P(),
        P(("dp", "tensor"), None),
    )
    return jax.shard_map(
        shards,
        mesh=mesh,
        in_specs=placed,
        out_specs=(
            P(("dp", "tensor"), None),
            P(("dp", "tensor"), None),
            P(None, "dp", None, "tensor"),
            P(),
            P(None, "tensor", "dp"),
            P(),
            P(None, "dp", "tensor"),
            P(),
            P(None, "tensor", "dp"),
            P(),
            P(),
            P(),
        ),
        check_vma=False,
    )
```

profile of v0, /device:TPU:1, one launch (start us, length us, event | category | flops | bytes accessed | tf_op | source)
XLA Modules:
  0.0 1549.2 jit_solution(5029799539793762543)
XLA Ops:
  10.5 25.2 %all-gather = bf16[1,1024,3,128]{3,1,2,0:T(8,128)(2,1)S(1)} all-gather(bf16[1,64,3,128]{3,1,2,0:T(8,128)(2,1)S(1)} %get-tuple-element.101), channel_id=2, replica_groups=mesh['dp'=16,'tensor'=8] {'dp'}, dimensions={1}, use_global_device_ids=true | all-gather | bytes 835584 | tf_op jit(solution)/shard_map/all_gather | solution.py:142
  36.1 17.0 %all-gather.1 = bf16[1,128,1024]{1,2,0:T(8,128)(2,1)S(1)} all-gather(bf16[1,128,64]{1,2,0:T(8,128)(2,1)S(1)} %get-tuple-element.103), channel_id=3, replica_groups=mesh['dp'=16,'tensor'=8] {'dp'}, dimensions={2}, use_global_device_ids=true | all-gather | bytes 278528 | tf_op jit(solution)/shard_map/all_gather | solution.py:143
  53.9 14.2 all-gather.21.cloned.1.call-done
  68.1 2.6 fusion.119
  81.3 71.1 %reduce-scatter.10.cloned.1.call-done = bf16[128,1024]{1,0:T(8,128)(2,1)} async-done(((bf16[1024,1024]{1,0:T(8,128)(2,1)}), bf16[128,1024]{1,0:T(8,128)(2,1)}) %reduce-scatter.10.cloned.1.call-update) | async-done | bytes 262160 | tf_op jit(solution)/shard_map/reduce_scatter | solution.py:111
  157.9 52.0 %all-gather.23.cloned.1.call-done = bf16[1024,1024]{1,0:T(8,128)(2,1)} async-done(((bf16[128,1024]{1,0:T(8,128)(2,1)}), bf16[1024,1024]{1,0:T(8,128)(2,1)}) %all-gather.23.cloned.1.call-update) | async-done | bytes 2097168 | tf_op jit(solution)/shard_map/all_gather | solution.py:101
  209.9 8.5 multiply_convert_fusion.3
  218.4 25.3 %all-gather.39.cloned.1.call-done = bf16[1,512,1024]{1,2,0:T(8,128)(2,1)} async-done(((bf16[1,512,64]{1,2,0:T(8,128)(2,1)}), bf16[1,512,1024]{1,2,0:T(8,128)(2,1)}) %all-gather.39.cloned.1.call-update) | async-done | bytes 1048592 | tf_op jit(solution)/shard_map/all_gather | solution.py:145
  243.7 3.9 convolution_convert_fusion.3
  248.3 72.8 %reduce-scatter.12.cloned.1.call-done = bf16[128,1024]{1,0:T(8,128)(2,1)} async-done(((bf16[1024,1024]{1,0:T(8,128)(2,1)}), bf16[128,1024]{1,0:T(8,128)(2,1)}) %reduce-scatter.12.cloned.1.call-update) | async-done | bytes 262160 | tf_op jit(solution)/shard_map/reduce_scatter | solution.py:111
  323.5 23.0 %all-gather.4 = bf16[1,1024,3,128]{3,1,2,0:T(8,128)(2,1)S(1)} all-gather(bf16[1,64,3,128]{3,1,2,0:T(8,128)(2,1)S(1)} %get-tuple-element.100), channel_id=6, replica_groups=mesh['dp'=16,'tensor'=8] {'dp'}, dimensions={1}, use_global_device_ids=true | all-gather | bytes 835584 | tf_op jit(solution)/shard_map/all_gather | solution.py:142
  346.8 17.1 %all-gather.5 = bf16[1,128,1024]{1,2,0:T(8,128)(2,1)S(1)} all-gather(bf16[1,128,64]{1,2,0:T(8,128)(2,1)S(1)} %get-tuple-element.102), channel_id=7, replica_groups=mesh['dp'=16,'tensor'=8] {'dp'}, dimensions={2}, use_global_device_ids=true | all-gather | bytes 278528 | tf_op jit(solution)/shard_map/all_gather | solution.py:143
  363.9 14.2 all-gather.25.cloned.1.call-done
  378.1 2.6 fusion.120
  391.5 71.1 %reduce-scatter.14.cloned.1.call-done = bf16[128,1024]{1,0:T(8,128)(2,1)} async-done(((bf16[1024,1024]{1,0:T(8,128)(2,1)}), bf16[128,1024]{1,0:T(8,128)(2,1)}) %reduce-scatter.14.cloned.1.call-update) | async-done | bytes 262160 | tf_op jit(solution)/shard_map/reduce_scatter | solution.py:111
  465.9 52.5 %all-gather.27.cloned.1.call-done = bf16[1024,1024]{1,0:T(8,128)(2,1)} async-done(((bf16[128,1024]{1,0:T(8,128)(2,1)}), bf16[1024,1024]{1,0:T(8,128)(2,1)}) %all-gather.27.cloned.1.call-update) | async-done | bytes 2097168 | tf_op jit(solution)/shard_map/all_gather | solution.py:101
  518.4 8.5 multiply_convert_fusion.2
  527.0 25.2 %all-gather.43.cloned.1.call-done = bf16[1,512,1024]{1,2,0:T(8,128)(2,1)} async-done(((bf16[1,512,64]{1,2,0:T(8,128)(2,1)}), bf16[1,512,1024]{1,2,0:T(8,128)(2,1)}) %all-gather.43.cloned.1.call-update) | async-done | bytes 1048592 | tf_op jit(solution)/shard_map/all_gather | solution.py:145
  552.2 3.9 convolution_convert_fusion.2
  556.1 73.2 %reduce-scatter.16.cloned.1.call-done = bf16[128,1024]{1,0:T(8,128)(2,1)} async-done(((bf16[1024,1024]{1,0:T(8,128)(2,1)}), bf16[128,1024]{1,0:T(8,128)(2,1)}) %reduce-scatter.16.cloned.1.call-update) | async-done | bytes 262160 | tf_op jit(solution)/shard_map/reduce_scatter | solution.py:111
  633.9 53.3 %all-gather.29.cloned.1.call-done = bf16[1024,1024]{1,0:T(8,128)(2,1)} async-done(((bf16[128,1024]{1,0:T(8,128)(2,1)}), bf16[1024,1024]{1,0:T(8,128)(2,1)}) %all-gather.29.cloned.1.call-update) | async-done | bytes 2097168 | tf_op jit(solution)/shard_map/all_gather | solution.py:104
  687.2 5.2 convert_reduce_fusion
  693.4 2.6 convolution_convert_fusion.1
  696.1 72.1 %reduce-scatter.18.cloned.1.call-done = bf16[128,1024]{1,0:T(8,128)(2,1)} async-done(((bf16[1024,1024]{1,0:T(8,128)(2,1)}), bf16[128,1024]{1,0:T(8,128)(2,1)}) %reduce-scatter.18.cloned.1.call-update) | async-done | bytes 262160 | tf_op jit(solution)/shard_map/reduce_scatter | solution.py:125
  771.8 53.1 %all-gather.31.cloned.1.call-done = bf16[1024,1024]{1,0:T(8,128)(2,1)} async-done(((bf16[128,1024]{1,0:T(8,128)(2,1)}), bf16[1024,1024]{1,0:T(8,128)(2,1)}) %all-gather.31.cloned.1.call-update) | async-done | bytes 2097168 | tf_op jit(solution)/shard_map/all_gather | solution.py:104
  827.4 4.9 fusion.44
  832.3 4.5 multiply_reduce_fusion.1
  842.2 3.9 bitcast_convert_fusion.1
  846.2 72.1 %reduce-scatter.20.cloned.1.call-done = bf16[128,1024]{1,0:T(8,128)(2,1)} async-done(((bf16[1024,1024]{1,0:T(8,128)(2,1)}), bf16[128,1024]{1,0:T(8,128)(2,1)}) %reduce-scatter.20.cloned.1.call-update) | async-done | bytes 262160 | tf_op jit(solution)/shard_map/reduce_scatter | solution.py:125
  921.8 53.3 %all-gather.33.cloned.1.call-done = bf16[1024,1024]{1,0:T(8,128)(2,1)} async-done(((bf16[128,1024]{1,0:T(8,128)(2,1)}), bf16[1024,1024]{1,0:T(8,128)(2,1)}) %all-gather.33.cloned.1.call-update) | async-done | bytes 2097168 | tf_op jit(solution)/shard_map/all_gather | solution.py:104
  975.1 5.2 convert_reduce_fusion.1
  981.3 2.6 convolution_convert_fusion
  984.0 72.0 %reduce-scatter.22.cloned.1.call-done = bf16[128,1024]{1,0:T(8,128)(2,1)} async-done(((bf16[1024,1024]{1,0:T(8,128)(2,1)}), bf16[128,1024]{1,0:T(8,128)(2,1)}) %reduce-scatter.22.cloned.1.call-update) | async-done | bytes 262160 | tf_op jit(solution)/shard_map/reduce_scatter | solution.py:125
  1059.6 4.3 fusion.37
  1073.6 2.6 fusion.36
  1076.5 4.1 copy.99
  1080.6 32.3 %all-gather.35.cloned.1.call-done = bf16[1024,1024]{1,0:T(8,128)(2,1)} async-done(((bf16[128,1024]{1,0:T(8,128)(2,1)}), bf16[1024,1024]{1,0:T(8,128)(2,1)}) %all-gather.35.cloned.1.call-update) | async-done | bytes 2097168 | tf_op jit(solution)/shard_map/all_gather | solution.py:104
  1118.8 4.9 fusion.47
  1123.9 4.4 multiply_reduce_fusion
  1128.3 4.7 multiply_convert_fusion
  1135.2 3.6 fusion.53
  1139.0 2.7 fusion.41
  1141.9 3.0 copy.97
  1146.0 2.6 bitcast_convert_fusion
  1152.1 21.3 %reduce-scatter.26.cloned.1.call-done = bf16[2,64,512]{2,1,0:T(8,128)(2,1)} async-done(((bf16[2,1024,512]{2,1,0:T(8,128)(2,1)}), bf16[2,64,512]{2,1,0:T(8,128)(2,1)}) %reduce-scatter.26.cloned.1.call-update) | async-done | bytes 131088 | tf_op jit(solution)/shard_map/reduce_scatter | solution.py:314
  1177.7 129.3 %all-reduce.10.cloned.1.call-done = (bf16[2,1024,3,128]{3,0,2,1:T(2,128)(2,1)}, bf16[2,128,1024]{1,0,2:T(2,128)(2,1)}, bf16[2,512,1024]{1,0,2:T(2,128)(2,1)}) async-done(((bf16[2,1024,3,128]{3,0,2,1:T(2,128)(2,1)}, bf16[2,128,1024]{1,0,2:T(2,128)(2,1)}, bf16[2,512,1024]{1,0,2:T(2,128)(2,1)}), (bf16[2,1024,3,128]{3,0,2,1:T(2,128)(2,1)}, bf16[2,128,1024]{1,0,2:T(2,128)(2,1)}, ...) | async-done | bytes 4194320
  1309.0 76.9 %reduce-scatter.24.cloned.1.call-done = bf16[128,1024]{1,0:T(8,128)(2,1)} async-done(((bf16[1024,1024]{1,0:T(8,128)(2,1)}), bf16[128,1024]{1,0:T(8,128)(2,1)}) %reduce-scatter.24.cloned.1.call-update) | async-done | bytes 262160 | tf_op jit(solution)/shard_map/reduce_scatter | solution.py:125
  1390.5 142.7 %all-reduce.8.cloned.1.call-done = (f32[2,2,1024]{2,1,0:T(2,128)}, f32[2,1024]{1,0:T(2,128)}, f32[2,4096]{1,0:T(2,128)}, f32[2,1024]{1,0:T(2,128)}, f32[2,2,1024]{2,1,0:T(2,128)}, /*index=5*/f32[2,2,1024]{2,1,0:T(2,128)}) async-done(((f32[2,2,1024]{2,1,0:T(2,128)}, f32[2,1024]{1,0:T(2,128)}, f32[2,4096]{1,0:T(2,128)}, f32[2,1024]{1,0:T(2,128)}, f32[2,2,1024]{2,1,0:T(2,128)}, ...) | async-done | bytes 98320 | tf_op jit(solution)/shard_map/psum | solution.py:324
  (292 shorter events, 103.2 us)
Async XLA Ops:
  8.0 28.0 %copy-start.42 = (bf16[2,2,1024]{2,1,0:T(2,128)(2,1)S(1)}, bf16[2,2,1024]{2,1,0:T(2,128)(2,1)}, u32[]{:S(2)}) copy-start(bf16[2,2,1024]{2,1,0:T(2,128)(2,1)} %param.16) | copy-start | bytes 24580
  8.0 28.1 %copy-start.37 = (bf16[2,128,64]{1,2,0:T(8,128)(2,1)S(1)}, bf16[2,128,64]{1,2,0:T(8,128)(2,1)}, u32[]{:S(2)}) copy-start(bf16[2,128,64]{1,2,0:T(8,128)(2,1)} %param.17) | copy-start | bytes 98308
  8.0 60.1 %all-gather.21.cloned.1.call-start = ((), (), s32[]{:S(2)}) async-start(), calls=%async_computation.9 | async-start | bytes 2359296 | tf_op jit(solution)/shard_map/all_gather | solution.py:101
  8.8 143.7 %reduce-scatter.10.cloned.1.call-start = ((), (), s32[]{:S(2)}) async-start(), calls=%async_computation.10 | async-start | bytes 2359296 | tf_op jit(solution)/shard_map/reduce_scatter | solution.py:111
  35.6 35.1 %copy-start.10 = (bf16[1,1024,3,128]{3,1,2,0:T(8,128)(2,1)}, bf16[1,1024,3,128]{3,1,2,0:T(8,128)(2,1)S(1)}, u32[]{:S(2)}) copy-start(bf16[1,1024,3,128]{3,1,2,0:T(8,128)(2,1)S(1)} %all-gather) | copy-start | bytes 2359300
  53.1 24.5 %copy-start.13 = (bf16[1,128,1024]{1,2,0:T(8,128)(2,1)}, bf16[1,128,1024]{1,2,0:T(8,128)(2,1)S(1)}, u32[]{:S(2)}) copy-start(bf16[1,128,1024]{1,2,0:T(8,128)(2,1)S(1)} %all-gather.1) | copy-start | bytes 786436
  53.9 17.0 %copy-start.27 = (pred[1024,1024]{0,1:T(8,128)(4,1)}, pred[1024,1024]{0,1:T(8,128)(4,1)S(1)}, u32[]{:S(2)}) copy-start(pred[1024,1024]{0,1:T(8,128)(4,1)S(1)} %broadcast_compare_fusion) | copy-start | bytes 3145732
  78.3 74.2 %copy-start.3 = (bf16[128,1024]{1,0:T(8,128)(2,1)S(1)}, bf16[128,1024]{1,0:T(8,128)(2,1)}, u32[]{:S(2)}) copy-start(bf16[128,1024]{1,0:T(8,128)(2,1)} %param.13) | copy-start | bytes 786436
  80.4 76.2 %copy-start.35 = (bf16[2,512,64]{1,2,0:T(8,128)(2,1)S(1)}, bf16[2,512,64]{1,2,0:T(8,128)(2,1)}, u32[]{:S(2)}) copy-start(bf16[2,512,64]{1,2,0:T(8,128)(2,1)} %param.21) | copy-start | bytes 393220
  80.4 77.4 %copy-start.36 = (bf16[2,4096]{1,0:T(2,128)(2,1)S(1)}, bf16[2,4096]{1,0:T(2,128)(2,1)}, u32[]{:S(2)}) copy-start(bf16[2,4096]{1,0:T(2,128)(2,1)} %param.20) | copy-start | bytes 49156
  80.4 77.5 %all-gather.37.cloned.1.call-start = ((), (), s32[]{:S(2)}) async-start(), calls=%async_computation.26 | async-start | bytes 1114112 | tf_op jit(solution)/shard_map/all_gather | solution.py:144
  81.2 128.8 %all-gather.23.cloned.1.call-start = ((), (), s32[]{:S(2)}) async-start(), calls=%async_computation.11 | async-start | bytes 2359296 | tf_op jit(solution)/shard_map/all_gather | solution.py:101
  156.6 87.1 %all-gather.39.cloned.1.call-start = ((), (), s32[]{:S(2)}) async-start(), calls=%async_computation.27 | async-start | bytes 1114112 | tf_op jit(solution)/shard_map/all_gather | solution.py:145
  157.3 163.7 %reduce-scatter.12.cloned.1.call-start = ((), (), s32[]{:S(2)}) async-start(), calls=%async_computation.12 | async-start | bytes 2359296 | tf_op jit(solution)/shard_map/reduce_scatter | solution.py:111
  218.4 25.3 %copy-start.31 = (bf16[1024,512]{1,0:T(8,128)(2,1)}, bf16[1024,512]{1,0:T(8,128)(2,1)S(1)}, u32[]{:S(2)}) copy-start(bf16[1024,512]{1,0:T(8,128)(2,1)S(1)} %get-tuple-element.93) | copy-start | bytes 3145732
  247.6 73.5 %copy-start.4 = (bf16[128,1024]{1,0:T(8,128)(2,1)S(1)}, bf16[128,1024]{1,0:T(8,128)(2,1)}, u32[]{:S(2)}) copy-start(bf16[128,1024]{1,0:T(8,128)(2,1)} %reduce-scatter.10.cloned.1.call-done) | copy-start | bytes 786436
  247.6 130.5 %all-gather.25.cloned.1.call-start = ((), (), s32[]{:S(2)}) async-start(), calls=%async_computation.13 | async-start | bytes 2359296 | tf_op jit(solution)/shard_map/all_gather | solution.py:101
  323.4 139.2 %reduce-scatter.14.cloned.1.call-start = ((), (), s32[]{:S(2)}) async-start(), calls=%async_computation.14 | async-start | bytes 2359296 | tf_op jit(solution)/shard_map/reduce_scatter | solution.py:111
  346.5 34.2 %copy-start.12 = (bf16[1,1024,3,128]{3,1,2,0:T(8,128)(2,1)}, bf16[1,1024,3,128]{3,1,2,0:T(8,128)(2,1)S(1)}, u32[]{:S(2)}) copy-start(bf16[1,1024,3,128]{3,1,2,0:T(8,128)(2,1)S(1)} %all-gather.4) | copy-start | bytes 2359300
  363.9 24.7 %copy-start.15 = (bf16[1,128,1024]{1,2,0:T(8,128)(2,1)}, bf16[1,128,1024]{1,2,0:T(8,128)(2,1)S(1)}, u32[]{:S(2)}) copy-start(bf16[1,128,1024]{1,2,0:T(8,128)(2,1)S(1)} %all-gather.5) | copy-start | bytes 786436
  390.7 75.2 %all-gather.41.cloned.1.call-start = ((), (), s32[]{:S(2)}) async-start(), calls=%async_computation.28 | async-start | bytes 1114112 | tf_op jit(solution)/shard_map/all_gather | solution.py:144
  391.5 127.0 %all-gather.27.cloned.1.call-start = ((), (), s32[]{:S(2)}) async-start(), calls=%async_computation.15 | async-start | bytes 2359296 | tf_op jit(solution)/shard_map/all_gather | solution.py:101
  465.1 87.2 %all-gather.43.cloned.1.call-start = ((), (), s32[]{:S(2)}) async-start(), calls=%async_computation.29 | async-start | bytes 1114112 | tf_op jit(solution)/shard_map/all_gather | solution.py:145
  465.6 163.7 %reduce-scatter.16.cloned.1.call-start = ((), (), s32[]{:S(2)}) async-start(), calls=%async_computation.16 | async-start | bytes 2359296 | tf_op jit(solution)/shard_map/reduce_scatter | solution.py:111
  527.0 25.3 %copy-start.32 = (bf16[1024,512]{1,0:T(8,128)(2,1)}, bf16[1024,512]{1,0:T(8,128)(2,1)S(1)}, u32[]{:S(2)}) copy-start(bf16[1024,512]{1,0:T(8,128)(2,1)S(1)} %get-tuple-element.87) | copy-start | bytes 3145732
  556.1 74.7 %copy-start.30 = (bf16[128,1024]{1,0:T(8,128)(2,1)S(1)}, bf16[128,1024]{1,0:T(8,128)(2,1)}, u32[]{:S(2)}) copy-start(bf16[128,1024]{1,0:T(8,128)(2,1)} %param.25) | copy-start | bytes 786436
  556.1 131.1 %all-gather.29.cloned.1.call-start = ((), (), s32[]{:S(2)}) async-start(), calls=%async_computation.17 | async-start | bytes 2359296 | tf_op jit(solution)/shard_map/all_gather | solution.py:104
  633.8 134.3 %reduce-scatter.18.cloned.1.call-start = ((), (), s32[]{:S(2)}) async-start(), calls=%async_computation.18 | async-start | bytes 2359296 | tf_op jit(solution)/shard_map/reduce_scatter | solution.py:125
  687.2 6.2 copy-start.47
  696.0 128.9 %all-gather.31.cloned.1.call-start = ((), (), s32[]{:S(2)}) async-start(), calls=%async_computation.19 | async-start | bytes 2359296 | tf_op jit(solution)/shard_map/all_gather | solution.py:104
  771.6 146.7 %reduce-scatter.20.cloned.1.call-start = ((), (), s32[]{:S(2)}) async-start(), calls=%async_computation.20 | async-start | bytes 2359296 | tf_op jit(solution)/shard_map/reduce_scatter | solution.py:125
  827.4 9.5 slice-start
  842.0 223.2 %copy-start.21 = (bf16[1024,1,128]{2,0,1:T(8,128)(2,1)}, bf16[1024,1,128]{2,0,1:T(8,128)(2,1)S(1)}, u32[]{:S(2)}) copy-start(bf16[1024,1,128]{2,0,1:T(8,128)(2,1)S(1)} %copy.83) | copy-start | bytes 786436
  842.2 223.0 %copy-start.23 = (bf16[1024,1,128]{2,0,1:T(8,128)(2,1)}, bf16[1024,1,128]{2,0,1:T(8,128)(2,1)S(1)}, u32[]{:S(2)}) copy-start(bf16[1024,1,128]{2,0,1:T(8,128)(2,1)S(1)} %copy.84) | copy-start | bytes 786436
  846.2 128.9 %all-gather.33.cloned.1.call-start = ((), (), s32[]{:S(2)}) async-start(), calls=%async_computation.21 | async-start | bytes 2359296 | tf_op jit(solution)/shard_map/all_gather | solution.py:104
  921.7 134.3 %reduce-scatter.22.cloned.1.call-start = ((), (), s32[]{:S(2)}) async-start(), calls=%async_computation.22 | async-start | bytes 2359296 | tf_op jit(solution)/shard_map/reduce_scatter | solution.py:125
  975.1 6.2 copy-start.46
  983.9 129.0 %all-gather.35.cloned.1.call-start = ((), (), s32[]{:S(2)}) async-start(), calls=%async_computation.23 | async-start | bytes 2359296 | tf_op jit(solution)/shard_map/all_gather | solution.py:104
  1059.5 113.9 %reduce-scatter.26.cloned.1.call-start = ((), (), s32[]{:S(2)}) async-start(), calls=%async_computation.25 | async-start | bytes 2228224 | tf_op jit(solution)/shard_map/reduce_scatter | solution.py:314
  1070.3 236.7 %all-reduce.10.cloned.1.call-start = ((), (), s32[]{:S(2)}) async-start(), calls=%async_computation.31 | async-start | bytes 8388608
  1076.5 36.4 %copy-start.18 = (bf16[2,64,1024]{2,1,0:T(8,128)(2,1)S(1)}, bf16[2,64,1024]{2,1,0:T(8,128)(2,1)}, u32[]{:S(2)}) copy-start(bf16[2,64,1024]{2,1,0:T(8,128)(2,1)} %copy-done.17) | copy-start | bytes 786436
  1080.6 37.4 %copy-start.14 = (bf16[1,128,1024]{1,2,0:T(8,128)(2,1)S(1)}, bf16[1,128,1024]{1,2,0:T(8,128)(2,1)}, u32[]{:S(2)}) copy-start(bf16[1,128,1024]{1,2,0:T(8,128)(2,1)} %copy-done.13) | copy-start | bytes 786436
  1112.9 5.1 copy-start.6
  1118.8 5.0 copy-start.8
  1139.0 6.0 copy-start.25
  1144.9 241.0 %reduce-scatter.24.cloned.1.call-start = ((), (), s32[]{:S(2)}) async-start(), calls=%async_computation.24 | async-start | bytes 2359296 | tf_op jit(solution)/shard_map/reduce_scatter | solution.py:125
  1148.6 28.2 %copy-start.26 = (bf16[1024,1,128]{2,0,1:T(8,128)(2,1)S(1)}, bf16[1024,1,128]{2,0,1:T(8,128)(2,1)}, u32[]{:S(2)}) copy-start(bf16[1024,1,128]{2,0,1:T(8,128)(2,1)} %copy-done.25) | copy-start | bytes 786436
  1148.7 384.5 %all-reduce.8.cloned.1.call-start = ((), (), s32[]{:S(2)}) async-start(), calls=%async_computation.30 | async-start | bytes 196608 | tf_op jit(solution)/shard_map/psum | solution.py:324
  (30 other events, 66.7 us)
Sparse Core Ops, SparseCore 0:
  11.2 56.8 all-gather.20
  80.6 71.8 reduce-scatter.9
  323.6 54.4 all-gather.24
  390.9 71.7 reduce-scatter.13
  556.2 73.0 reduce-scatter.15
  696.1 71.9 reduce-scatter.17
  846.3 71.9 reduce-scatter.19
  984.0 71.9 reduce-scatter.21
Sparse Core Ops, SparseCore 1:
  83.2 31.8 all-gather.36
  156.7 53.2 all-gather.22
  212.1 31.6 all-gather.38
  247.7 73.3 reduce-scatter.11
  393.8 31.8 all-gather.40
  465.1 53.3 all-gather.26
  520.6 31.6 all-gather.42
  633.9 53.2 all-gather.28
  771.6 53.2 all-gather.30
  921.8 53.2 all-gather.32
  1059.6 53.2 all-gather.34
  1115.3 58.0 reduce-scatter.25
  1176.0 131.0 all-reduce.9
  1310.7 75.1 reduce-scatter.23
  1392.9 140.2 all-reduce.7
where the time goes:
time: 1560 us; the launch traced here: 1550 us
  waiting for transfers between devices  1250 us (80%)
  matrix products  109 us (7%)
  blocking collectives  82.3 us (5%)
  other arithmetic  48.2 us (3%)
  local copies, waits for them, and re-layouts  37.2 us (2%)
  between operations  18 us (1%)
    reduce_scatter x4, waiting for transfers between devices, scatter_backward(): lax.psum_scatter(term_rows(jnp.int32(0), own_rows * lax.axis_size('tensor...  293 us
    reduce_scatter x4, waiting for transfers between devices, scatter_forward(): lax.psum_scatter(term_rows(jnp.int32(0), own_rows * lax.axis_size('tensor...  288 us
    all_gather x4, waiting for transfers between devices, gather_grads(): return lax.all_gather(values, 'tensor', axis=0, tiled=True)  192 us
    psum x1, waiting for transfers between devices, shards(): lax.psum((small_stacked[0], small_stacked[1], small_stacked[2], small_sta...  143 us
    all_gather x4, waiting for transfers between devices, gather_rows(): return lax.all_gather(values, 'tensor', axis=0, tiled=True)  133 us
    unnamed x24, waiting for transfers between devices  132 us
    all_gather x2, waiting for transfers between devices, shards(): lax.all_gather(w_down[layer_at], 'dp', axis=1, tiled=True)  50.5 us
    all_gather x2, blocking collectives, shards(): lax.all_gather(w_qkv[layer_at], 'dp', axis=0, tiled=True)  48.2 us
  transfers between devices with their start and end apart: 23, of which 21 were waited for; matrix products, arithmetic and copies ran while one was open for 6% of the time, Pallas kernels for 0%

commit v1 on v0

v1 whole, which is shorter than its diff:
```python
import functools

import jax
import jax.numpy as jnp
from jax import lax
from jax.experimental import pallas as pl
from jax.experimental.pallas import tpu as pltpu
from jax.sharding import PartitionSpec as P

DH = 64
EPSILON = 1e-06
MESH = pl.DeviceIdType.MESH
F32 = jnp.float32
BF16 = jnp.bfloat16


def place():
    dp, tensor = lax.axis_index("dp"), lax.axis_index("tensor")
    core = lax.rem(dp, 2)
    z = lax.rem(lax.div(dp, 2), 4)
    x = lax.rem(lax.div(tensor, 4) * 2 + lax.div(dp, 8), 4)
    y = lax.rem(tensor, 4)
    return x, y, z, core


def device(x, y, z, core):
    x, y, z = lax.rem(x, 4), lax.rem(y, 4), lax.rem(z, 4)
    return (lax.rem(x, 2) * 8 + z * 2 + core, lax.div(x, 2) * 4 + y)


def block_of(x, z):
    x, z = lax.rem(x, 4), lax.rem(z, 4)
    return lax.rem(x, 2) * 8 + z * 2 + lax.div(x, 2)


def greet(devices):
    barrier = pltpu.get_barrier_semaphore()
    for other in devices:
        pl.semaphore_signal(barrier, inc=1, device_id=other, device_id_type=MESH)
    pl.semaphore_wait(barrier, len(devices))


class Copies:
    def __init__(self, send, recv):
        self.send, self.recv, self.started = send, recv, []

    def start(self, src, dst, to):
        at = len(self.started)
        copy = pltpu.make_async_remote_copy(
            src_ref=src,
            dst_ref=dst,
            send_sem=self.send.at[at],
            recv_sem=self.recv.at[at],
            device_id=to,
            device_id_type=MESH,
        )
        copy.start()
        self.started.append(copy)
        return copy

    def wait_sends(self):
        for copy in self.started:
            copy.wait_send()


def group_neighbours():
    x, y, z, core = place()
    return (
        device(x, y, z, 1 - core),
        device(x, y + 1, z, core),
        device(x, y + 3, z, core),
    )


GATHER_COPIES = 12
SCATTER_COPIES = 10


def gather_group(copies, out):
    x, y, z, core = place()
    pair, after, before = group_neighbours()
    half = out.shape[1] // 2
    top, low = pl.ds(0, half), pl.ds(half, half)
    here = core * 4

    def part(step, rows):
        return out.at[here + lax.rem(y + step, 4), rows]

    def send(step, rows, to):
        return copies.start(part(step, rows), part(step, rows), to)

    top_after = send(0, top, after)
    low_before = send(0, low, before)
    low_after = send(0, low, after)
    top_before = send(0, top, before)
    everything = pl.ds(0, 2 * half)
    own_pair = send(0, everything, pair)
    top_after.wait_recv()
    far_top = send(3, top, after)
    low_before.wait_recv()
    far_low = send(1, low, before)
    low_after.wait_recv()
    pair_before = send(3, everything, pair)
    top_before.wait_recv()
    pair_after = send(1, everything, pair)
    far_top.wait_recv()
    pair_top = send(2, top, pair)
    far_low.wait_recv()
    pair_low = send(2, low, pair)
    for copy in (own_pair, pair_before, pair_after, pair_top, pair_low):
        copy.wait_recv()


def scatter_group(copies, part, from_pair, staged, far, near):
    x, y, z, core = place()
    pair, after, before = group_neighbours()
    half = part.shape[1] // 2
    top, low = pl.ds(0, half), pl.ds(half, half)
    here, there = core * 4, (1 - core) * 4
    steps = (2, 1, 3, 0)
    swaps = [
        copies.start(part.at[there + lax.rem(y + step, 4)], from_pair.at[slot], pair)
        for slot, step in enumerate(steps)
    ]

    def chip(slot, rows):
        own = part[here + lax.rem(y + steps[slot], 4), rows].astype(F32)
        return own + from_pair[slot, rows].astype(F32)

    swaps[0].wait_recv()
    staged[0, top] = chip(0, top).astype(BF16)
    far_top = copies.start(staged.at[0, top], far.at[top], after)
    staged[0, low] = chip(0, low).astype(BF16)
    far_low = copies.start(staged.at[0, low], far.at[low], before)
    swaps[1].wait_recv()
    staged[1, low] = chip(1, low).astype(BF16)
    low_after = copies.start(staged.at[1, low], near.at[0, low], after)
    swaps[2].wait_recv()
    staged[2, top] = chip(2, top).astype(BF16)
    top_before = copies.start(staged.at[2, top], near.at[1, top], before)
    far_top.wait_recv()
    staged[1, top] = (chip(1, top) + far[top].astype(F32)).astype(BF16)
    top_after = copies.start(staged.at[1, top], near.at[0, top], after)
    far_low.wait_recv()
    staged[2, low] = (chip(2, low) + far[low].astype(F32)).astype(BF16)
    low_before = copies.start(staged.at[2, low], near.at[1, low], before)
    swaps[3].wait_recv()
    own = chip(3, pl.ds(0, 2 * half))
    for copy in (low_after, top_before, top_after, low_before):
        copy.wait_recv()
    return own + near[0].astype(F32) + near[1].astype(F32)


def scatter_scratch(rows, width):
    return [
        pltpu.VMEM((4, rows, width), BF16),
        pltpu.VMEM((3, rows, width), BF16),
        pltpu.VMEM((rows, width), BF16),
        pltpu.VMEM((2, rows, width), BF16),
    ]


def sems(count):
    return [pltpu.SemaphoreType.DMA((count,)), pltpu.SemaphoreType.DMA((count,))]


def plane_ring(axis):
    x, y, z, core = place()
    if axis == "x":
        return device(x + 1, y, z, core), device(x + 3, y, z, core)
    return device(x, y, z + 1, core), device(x, y, z + 3, core)


def plane_at(first, u, v):
    return block_of(u, v) if first == "x" else block_of(v, u)


PLANE_GATHER_COPIES = 36
PLANE_SCATTER_COPIES = 36


def gather_plane(copies, out):
    x, y, z, core = place()
    quarter = out.shape[1] // 4
    paths = []
    for first, base in (("x", 0), ("z", 2 * quarter)):
        v, u = (x, z) if first == "x" else (z, x)
        other = "z" if first == "x" else "x"
        paths.append(
            dict(
                first=first,
                v=v,
                u=u,
                ring=plane_ring(first),
                cross=plane_ring(other),
                halves=(pl.ds(base, quarter), pl.ds(base + quarter, quarter)),
                whole=pl.ds(base, 2 * quarter),
            )
        )

    def send(path, dv, du, rows, to):
        at = plane_at(path["first"], path["v"] + dv, path["u"] + du)
        return copies.start(out.at[at, rows], out.at[at, rows], to)

    for path in paths:
        after, before = path["ring"]
        top, low = path["halves"]
        path["ta"] = send(path, 0, 0, top, after)
        path["lb"] = send(path, 0, 0, low, before)
        path["la"] = send(path, 0, 0, low, after)
        path["tb"] = send(path, 0, 0, top, before)
        path["c"] = {0: [send(path, 0, 0, path["whole"], to) for to in path["cross"]]}
    for path in paths:
        path["ta"].wait_recv()
        path["ft"] = send(path, 3, 0, path["halves"][0], path["ring"][0])
        path["lb"].wait_recv()
        path["fl"] = send(path, 1, 0, path["halves"][1], path["ring"][1])
    for path in paths:
        path["la"].wait_recv()
        path["c"][3] = [send(path, 3, 0, path["whole"], to) for to in path["cross"]]
        path["tb"].wait_recv()
        path["c"][1] = [send(path, 1, 0, path["whole"], to) for to in path["cross"]]
    last = []
    for path in paths:
        path["c"][0][0].wait_recv()
        last.append(send(path, 0, 3, path["whole"], path["cross"][0]))
    for path in paths:
        path["ft"].wait_recv()
        path["fl"].wait_recv()
        path["c"][2] = [send(path, 2, 0, path["whole"], to) for to in path["cross"]]
    for path in paths:
        path["c"][3][0].wait_recv()
        last.append(send(path, 3, 3, path["whole"], path["cross"][0]))
        path["c"][1][1].wait_recv()
        last.append(send(path, 1, 1, path["whole"], path["cross"][1]))
    for path in paths:
        path["c"][2][1].wait_recv()
        last.append(send(path, 2, 1, path["whole"], path["cross"][1]))
    for path in paths:
        for copy in (path["c"][0][1], path["c"][3][1], path["c"][1][0], path["c"][2][0]):
            copy.wait_recv()
    for copy in last:
        copy.wait_recv()


def scatter_plane_scratch(rows, width):
    half = rows // 2
    return [
        pltpu.VMEM((2, 4, half, width), BF16),
        pltpu.VMEM((2, 2, 4, half, width), BF16),
        pltpu.VMEM((2, 4, half, width), BF16),
        pltpu.VMEM((2, 4, half, width), BF16),
        pltpu.VMEM((2, half, width), BF16),
        pltpu.VMEM((2, 2, half, width), BF16),
        pltpu.VMEM((2, 2, half // 2, width), BF16),
    ]


def scatter_plane(copies, part, out, far, near, passed, summed, far2, near2, passed2):
    x, y, z, core = place()
    half = part.shape[1] // 2
    quarter = half // 2
    paths = []
    for at, (first, base) in enumerate((("x", 0), ("z", half))):
        u, v = (x, z) if first == "x" else (z, x)
        other = "z" if first == "x" else "x"
        paths.append(
            dict(
                at=at,
                first=first,
                u=u,
                v=v,
                ring=plane_ring(first),
                cross=plane_ring(other),
                rows=pl.ds(base, half),
                base=base,
            )
        )

    def source(path, du, v):
        return (plane_at(path["first"], path["u"] + du, v), path["rows"])

    for path in paths:
        at, (after, before) = path["at"], path["ring"]
        path["far"] = [
            copies.start(
                part.at[source(path, 2, v)], far.at[at, v], after if v < 2 else before
            )
            for v in range(4)
        ]
    for path in paths:
        at, (after, before) = path["at"], path["ring"]
        path["near"] = [
            copies.start(part.at[source(path, 1, v)], near.at[at, 0, v], after) for v in (2, 3)
        ] + [
            copies.start(part.at[source(path, 3, v)], near.at[at, 1, v], before) for v in (0, 1)
        ]
    for path in paths:
        at, (after, before) = path["at"], path["ring"]
        for v in (0, 2, 1, 3):
            path["far"][v].wait_recv()
            du, slot, to = (1, 0, after) if v < 2 else (3, 1, before)
            own = part[source(path, du, v)].astype(F32)
            passed[at, v] = (own + far[at, v].astype(F32)).astype(BF16)
            path["near"].append(copies.start(passed.at[at, v], near.at[at, slot, v], to))
    for path in paths:
        at = path["at"]
        for copy in path["near"]:
            copy.wait_recv()
        for v in range(4):
            own = part[source(path, 0, v)].astype(F32)
            summed[at, v] = (
                own + near[at, 0, v].astype(F32) + near[at, 1, v].astype(F32)
            ).astype(BF16)
        v, (after, before) = path["v"], path["cross"]
        top, low = pl.ds(0, quarter), pl.ds(quarter, quarter)
        v1, v2, v3 = lax.rem(v + 1, 4), lax.rem(v + 2, 4), lax.rem(v + 3, 4)
        path["ft"] = copies.start(summed.at[at, v2, top], far2.at[at, top], after)
        path["fl"] = copies.start(summed.at[at, v2, low], far2.at[at, low], before)
        path["last"] = [
            copies.start(summed.at[at, v1, low], near2.at[at, 0, low], after),
            copies.start(summed.at[at, v3, top], near2.at[at, 1, top], before),
        ]
    for path in paths:
        at, v, (after, before) = path["at"], path["v"], path["cross"]
        top, low = pl.ds(0, quarter), pl.ds(quarter, quarter)
        v1, v3 = lax.rem(v + 1, 4), lax.rem(v + 3, 4)
        path["ft"].wait_recv()
        passed2[at, 0] = (summed[at, v1, top].astype(F32) + far2[at, top].astype(F32)).astype(BF16)
        path["last"].append(copies.start(passed2.at[at, 0], near2.at[at, 0, top], after))
        path["fl"].wait_recv()
        passed2[at, 1] = (summed[at, v3, low].astype(F32) + far2[at, low].astype(F32)).astype(BF16)
        path["last"].append(copies.start(passed2.at[at, 1], near2.at[at, 1, low], before))
    for path in paths:
        at, v = path["at"], path["v"]
        for copy in path["last"]:
            copy.wait_recv()
        total = summed[at, v].astype(F32) + near2[at, 0].astype(F32) + near2[at, 1].astype(F32)
        out[path["rows"]] = total


def params(number):
    return pltpu.CompilerParams(
        collective_id=number, has_side_effects=True, vmem_limit_bytes=48 * 2**20
    )


VMEM = pl.BlockSpec(memory_space=pltpu.VMEM)


def start_kernel(tokens, weights, rows_out, weights_out, send, recv, wsend, wrecv):
    x, y, z, core = place()
    greet([*group_neighbours(), *plane_ring("x"), *plane_ring("z")])
    weights_out[block_of(x, z)] = weights[...]
    rows_out[core * 4 + y] = tokens[...]
    plane, group = Copies(wsend, wrecv), Copies(send, recv)
    gather_group(group, rows_out)
    gather_plane(plane, weights_out)
    group.wait_sends()
    plane.wait_sends()


def start(tokens, weights):
    rows, width = tokens.shape
    held, columns = weights.shape
    gathered, full = pl.pallas_call(
        start_kernel,
        out_shape=(
            jax.ShapeDtypeStruct((8, rows, width), BF16),
            jax.ShapeDtypeStruct((16, held, columns), BF16),
        ),
        in_specs=[VMEM] * 2,
        out_specs=(VMEM, VMEM),
        scratch_shapes=sems(GATHER_COPIES) + sems(PLANE_GATHER_COPIES),
        compiler_params=params(0),
        name="start",
    )(tokens, weights)
    return gathered.reshape(8 * rows, width), full.reshape(16 * held, columns)


def normed_parts(stream):
    row_mean = jnp.mean(stream, axis=-1, keepdims=True)
    centered = stream - row_mean
    row_var = jnp.mean(centered * centered, axis=-1, keepdims=True)
    scale = lax.rsqrt(row_var + EPSILON)
    return centered * scale, scale


def norm_pull(unit, scale, gain, grad, sums):
    scaled = grad * gain
    inner = jnp.mean(scaled * unit, axis=-1, keepdims=True)
    pulled = scale * (scaled - jnp.mean(scaled, axis=-1, keepdims=True) - unit * inner)
    low = pulled.astype(BF16)
    sums[0:1] = jnp.sum(grad * unit, axis=0, keepdims=True)
    sums[1:2] = jnp.sum(grad, axis=0, keepdims=True)
    sums[2:3] = jnp.sum(low.astype(F32), axis=0, keepdims=True)
    return pulled, low


def forward_kernel(
    part, held, vectors, stream_out, normed_out, rows_out,
    from_pair, staged, far, near, send, recv, gsend, grecv,
):
    x, y, z, core = place()
    greet(group_neighbours())
    scatter, gather = Copies(send, recv), Copies(gsend, grecv)
    total = scatter_group(scatter, part, from_pair, staged, far, near)
    stream = held[...] + total + vectors[0:1]
    stream_out[...] = stream
    unit, _ = normed_parts(stream)
    normed = unit * vectors[1:2] + vectors[2:3]
    normed_out[...] = normed
    rows_out[core * 4 + y] = normed.astype(BF16)
    gather_group(gather, rows_out)
    scatter.wait_sends()
    gather.wait_sends()


def turn_kernel(
    part, held, vectors, grad, encoded_out, pulled_out, sums_out, rows_out,
    from_pair, staged, far, near, send, recv, gsend, grecv,
):
    x, y, z, core = place()
    greet(group_neighbours())
    scatter, gather = Copies(send, recv), Copies(gsend, grecv)
    total = scatter_group(scatter, part, from_pair, staged, far, near)
    stream = held[...] + total + vectors[0:1]
    unit, scale = normed_parts(stream)
    encoded_out[...] = (unit * vectors[1:2] + vectors[2:3]).astype(BF16)
    pulled, low = norm_pull(unit, scale, vectors[1:2], grad[...].astype(F32), sums_out)
    pulled_out[...] = pulled
    rows_out[core * 4 + y] = low
    gather_group(gather, rows_out)
    scatter.wait_sends()
    gather.wait_sends()


def backward_kernel(
    part, held, vectors, stream, pulled_out, sums_out, rows_out,
    from_pair, staged, far, near, send, recv, gsend, grecv,
):
    x, y, z, core = place()
    greet(group_neighbours())
    scatter, gather = Copies(send, recv), Copies(gsend, grecv)
    total = scatter_group(scatter, part, from_pair, staged, far, near)
    unit, scale = normed_parts(stream[...])
    pulled, low = norm_pull(unit, scale, vectors[1:2], held[...] + total, sums_out)
    pulled_out[...] = pulled
    rows_out[core * 4 + y] = low
    gather_group(gather, rows_out)
    scatter.wait_sends()
    gather.wait_sends()


def group_call(kernel, number, name, operands, outs):
    part = operands[0]
    rows, width = part.shape[0] // 8, part.shape[1]
    shapes = tuple(jax.ShapeDtypeStruct(shape, kind) for shape, kind in outs)
    shapes += (jax.ShapeDtypeStruct((8, rows, width), BF16),)
    results = pl.pallas_call(
        kernel,
        out_shape=shapes,
        in_specs=[VMEM] * len(operands),
        out_specs=(VMEM,) * len(shapes),
        scratch_shapes=scatter_scratch(rows, width)
        + sems(SCATTER_COPIES)
        + sems(GATHER_COPIES),
        compiler_params=params(number),
        name=name,
    )(part.reshape(8, rows, width), *operands[1:])
    return (*results[:-1], results[-1].reshape(8 * rows, width))


def end_kernel(
    part, held, grads, rows_out, grads_out,
    from_pair, staged, far, near, pfar, pnear, passed, summed, far2, near2, passed2,
    send, recv, psend, precv,
):
    greet([*group_neighbours(), *plane_ring("x"), *plane_ring("z")])
    group, plane = Copies(send, recv), Copies(psend, precv)
    total = scatter_group(group, part, from_pair, staged, far, near)
    rows_out[...] = (held[...] + total).astype(BF16)
    scatter_plane(plane, grads, grads_out, pfar, pnear, passed, summed, far2, near2, passed2)
    group.wait_sends()
    plane.wait_sends()


def end(part, held, grads):
    rows, width = held.shape
    kept, columns = grads.shape[0] // 16, grads.shape[1]
    return pl.pallas_call(
        end_kernel,
        out_shape=(
            jax.ShapeDtypeStruct((rows, width), BF16),
            jax.ShapeDtypeStruct((kept, columns), F32),
        ),
        in_specs=[VMEM] * 3,
        out_specs=(VMEM, VMEM),
        scratch_shapes=scatter_scratch(rows, width)
        + scatter_plane_scratch(kept, columns)
        + sems(SCATTER_COPIES)
        + sems(PLANE_SCATTER_COPIES),
        compiler_params=params(4),
        name="end",
    )(part.reshape(8, rows, width), held, grads.reshape(16, kept, columns))


def segment_ids(shard_lengths, total_rows, seq_count):
    seq_ends = jnp.cumsum(shard_lengths)
    positions = jnp.arange(total_rows, dtype=jnp.int32)
    segments = jnp.sum((positions[:, None] >= seq_ends[None, :]).astype(jnp.int32), axis=1)
    return jnp.where(segments == seq_count, seq_count + positions, segments)


def masked_scores(queries, keys_in, allowed, score_scale):
    scores = (
        jnp.einsum("qhd,khd->hqk", queries, keys_in, preferred_element_type=jnp.float32)
        * score_scale
    )
    return jnp.where(allowed[None], scores, -1e30)


def attend_forward(queries, keys_in, values_in, allowed, score_scale):
    scores = masked_scores(queries, keys_in, allowed, score_scale)
    row_peak = jnp.max(scores, axis=-1, keepdims=True)
    exp_scores = jnp.exp(scores - row_peak)
    row_total = jnp.sum(exp_scores, axis=-1, keepdims=True)
    attn_probs = (exp_scores / row_total).astype(jnp.bfloat16)
    context = jnp.einsum("hqk,khd->qhd", attn_probs, values_in, preferred_element_type=jnp.float32)
    return (context, row_peak + jnp.log(row_total))


def attend_backward(queries, keys_in, values_in, allowed, score_scale, log_total, grad_context):
    scores = masked_scores(queries, keys_in, allowed, score_scale)
    attn_probs = jnp.exp(scores - log_total)
    probs_low = attn_probs.astype(jnp.bfloat16)
    grad_probs = jnp.einsum(
        "qhd,khd->hqk", grad_context, values_in, preferred_element_type=jnp.float32
    )
    grad_values = jnp.einsum(
        "hqk,qhd->khd", probs_low, grad_context, preferred_element_type=jnp.float32
    )
    row_inner = jnp.sum(attn_probs * grad_probs, axis=-1, keepdims=True)
    grad_scores = (attn_probs * (grad_probs - row_inner)).astype(jnp.bfloat16)
    grad_queries = (
        jnp.einsum("hqk,khd->qhd", grad_scores, keys_in, preferred_element_type=jnp.float32)
        * score_scale
    )
    grad_keys = (
        jnp.einsum("hqk,qhd->khd", grad_scores, queries, preferred_element_type=jnp.float32)
        * score_scale
    )
    return (grad_queries, grad_keys, grad_values)


def exact_gelu(values):
    return jax.nn.gelu(values, approximate=False)


CONTRACT_LAST = (((1,), (1,)), ((), ()))
CONTRACT_FIRST = (((0,), (0,)), ((), ()))


def flat(x, y, z, core):
    return (x % 2 * 8 + z * 2 + core) * 8 + x // 2 * 4 + y


CHIPS = [(x, y, z, core) for x in range(4) for y in range(4) for z in range(4) for core in (0, 1)]
SWAP = [
    (flat(x, y, z, core), flat(core * 2 + x % 2, y, z, x // 2)) for x, y, z, core in CHIPS
]
PLANES = [
    [flat(xh * 2 + xl, y, z, core) for xl in (0, 1) for z in range(4) for xh in (0, 1)]
    for core in (0, 1)
    for y in range(4)
]
AXES = ("dp", "tensor")


def swap(values):
    return lax.ppermute(values, AXES, SWAP)


def shards(
    tokens,
    lengths,
    w_qkv,
    b_qv,
    w_out,
    b_out,
    w_in,
    b_in,
    w_down,
    b_down,
    ln_gain,
    ln_bias,
    cotangent,
):
    x, y, z, core = place()
    column = core * 4 + y
    own_rows, width = tokens.shape
    total_rows = own_rows * 8
    layers, kept = w_qkv.shape[:2]
    col_width = w_qkv.shape[3]
    hidden_width = w_in.shape[2]
    head_count = col_width // DH
    score_scale = DH ** (-0.5)
    cuts = (0, 3 * col_width, 4 * col_width, 4 * col_width + hidden_width)

    packed = [
        jnp.concatenate(
            [
                w_qkv[at].reshape(kept, 3 * col_width),
                w_out[at].T,
                w_in[at],
                w_down[at].T,
            ],
            axis=1,
        )
        for at in range(layers)
    ]
    first_weights = swap(packed[0])
    tokens = swap(tokens)
    lengths = swap(lengths)
    later_weights = swap(packed[1])
    cotangent = swap(cotangent)
    attn_input, full = start(tokens, first_weights)
    later = lax.all_gather(later_weights, AXES, axis_index_groups=PLANES, axis=0, tiled=True)
    weights = [full, later]

    segments = segment_ids(lengths[0], total_rows, lengths.shape[1])
    allowed = segments[:, None] == segments[None, :]

    def pieces(packed_weights):
        return (
            packed_weights[:, cuts[0] : cuts[1]],
            packed_weights[:, cuts[1] : cuts[2]],
            packed_weights[:, cuts[2] : cuts[3]],
            packed_weights[:, cuts[3] :],
        )

    def vectors(bias, at, which):
        rows = [bias.astype(F32), ln_gain[at, which].astype(F32), ln_bias[at, which].astype(F32)]
        return jnp.stack(rows + [jnp.zeros_like(rows[0])] * 5)

    row_kind = ((own_rows, width), F32)
    sum_kind = ((8, width), F32)
    low_kind = ((own_rows, width), BF16)
    hidden = tokens.astype(F32)
    stored = []
    for at in range(layers):
        full_qkv, full_out, full_in, full_down = pieces(weights[at])
        bias_qv = lax.dynamic_slice_in_dim(
            b_qv[at].astype(F32), column * col_width, col_width, 1
        )
        bias_all = jnp.concatenate([bias_qv[0], jnp.zeros_like(bias_qv[0]), bias_qv[1]])
        qkv = jnp.dot(attn_input, full_qkv, preferred_element_type=F32)
        qkv_low = (qkv + bias_all).astype(BF16)
        head_view = qkv_low.reshape(total_rows, 3, head_count, DH)
        context, log_total = attend_forward(
            head_view[:, 0], head_view[:, 1], head_view[:, 2], allowed, score_scale
        )
        context_low = context.reshape(total_rows, col_width).astype(BF16)
        branch = lax.dot_general(
            context_low, full_out, CONTRACT_LAST, preferred_element_type=F32
        ).astype(BF16)
        first_vectors = vectors(b_out[at], at, 0)
        first_sum, normed, mlp_input = group_call(
            forward_kernel, 1, "forward", (branch, hidden, first_vectors), (row_kind, row_kind)
        )
        bias_in = lax.dynamic_slice_in_dim(
            b_in[at].astype(F32), column * hidden_width, hidden_width, 0
        )
        pre_gelu = jnp.dot(mlp_input, full_in, preferred_element_type=F32) + bias_in
        act_low = exact_gelu(pre_gelu).astype(BF16)
        branch = lax.dot_general(
            act_low, full_down, CONTRACT_LAST, preferred_element_type=F32
        ).astype(BF16)
        second_vectors = vectors(b_down[at], at, 1)
        stored.append(
            [attn_input, qkv_low, log_total, context_low, first_sum, mlp_input, pre_gelu,
             act_low, first_vectors, second_vectors]
        )
        if at < layers - 1:
            second_sum, hidden, attn_input = group_call(
                forward_kernel, 1, "forward", (branch, normed, second_vectors), (row_kind, row_kind)
            )
            stored[at].append(second_sum)
        else:
            encoded, grad_second, sums_two, down_full = group_call(
                turn_kernel,
                2,
                "turn",
                (branch, normed, second_vectors, cotangent),
                (low_kind, row_kind, sum_kind),
            )

    weight_list = [None] * layers
    small_list = [None] * layers
    for at in reversed(range(layers)):
        (
            attn_input, qkv_low, log_total, context_low, first_sum, mlp_input, pre_gelu,
            act_low, first_vectors, second_vectors,
        ) = stored[at][:10]
        full_qkv, full_out, full_in, full_down = pieces(weights[at])
        grad_act = jnp.dot(down_full, full_down, preferred_element_type=F32)
        grad_w_down = lax.dot_general(
            down_full, act_low, CONTRACT_FIRST, preferred_element_type=F32
        )
        pre_low = jax.vjp(exact_gelu, pre_gelu)[1](grad_act)[0].astype(BF16)
        grad_w_in = lax.dot_general(
            mlp_input, pre_low, CONTRACT_FIRST, preferred_element_type=F32
        )
        branch = lax.dot_general(
            pre_low, full_in, CONTRACT_LAST, preferred_element_type=F32
        ).astype(BF16)
        grad_first, sums_one, attn_full = group_call(
            backward_kernel,
            3,
            "backward",
            (branch, grad_second, first_vectors, first_sum),
            (row_kind, sum_kind),
        )
        grad_context = jnp.dot(attn_full, full_out, preferred_element_type=F32)
        grad_context_low = grad_context.astype(BF16).reshape(total_rows, head_count, DH)
        grad_w_out = lax.dot_general(
            attn_full, context_low, CONTRACT_FIRST, preferred_element_type=F32
        )
        head_view = qkv_low.reshape(total_rows, 3, head_count, DH)
        grad_queries, grad_keys, grad_values = attend_backward(
            head_view[:, 0], head_view[:, 1], head_view[:, 2],
            allowed, score_scale, log_total, grad_context_low,
        )
        grad_qkv_low = (
            jnp.stack([grad_queries, grad_keys, grad_values], axis=1)
            .reshape(total_rows, 3 * col_width)
            .astype(BF16)
        )
        grad_w_qkv = lax.dot_general(
            attn_input, grad_qkv_low, CONTRACT_FIRST, preferred_element_type=F32
        )
        branch = lax.dot_general(
            grad_qkv_low, full_qkv, CONTRACT_LAST, preferred_element_type=F32
        ).astype(BF16)
        weight_grads = jnp.concatenate(
            [
                grad_w_qkv.astype(BF16),
                grad_w_out.astype(BF16),
                grad_w_in.astype(BF16),
                grad_w_down.astype(BF16),
            ],
            axis=1,
        )
        qkv_sums = jnp.sum(grad_qkv_low.astype(F32), axis=0).reshape(3, col_width)
        bias_qv_full = lax.dynamic_update_slice_in_dim(
            jnp.zeros((2, b_qv.shape[2]), F32),
            jnp.stack([qkv_sums[0], qkv_sums[2]]),
            column * col_width,
            1,
        )
        bias_in_full = lax.dynamic_update_slice_in_dim(
            jnp.zeros((b_in.shape[1],), F32),
            jnp.sum(pre_low.astype(F32), axis=0),
            column * hidden_width,
            0,
        )
        small_list[at] = jnp.concatenate(
            [
                bias_qv_full,
                bias_in_full.reshape(-1, width),
                sums_one[:3],
                sums_two[:3],
            ]
        )
        if at > 0:
            weight_list[at] = lax.psum_scatter(
                weight_grads, AXES, scatter_dimension=0, axis_index_groups=PLANES, tiled=True
            ).astype(F32)
            grad_second, sums_two, down_full = group_call(
                backward_kernel,
                3,
                "backward",
                (branch, grad_first, stored[at - 1][9], stored[at - 1][10]),
                (row_kind, sum_kind),
            )
        else:
            g_tokens, weight_list[at] = end(branch, grad_first, weight_grads)

    small = lax.psum(jnp.stack(small_list), AXES)
    grads = swap(jnp.stack(weight_list).astype(BF16)).astype(F32)
    g_qkv, g_out, g_in, g_down = (
        grads[:, :, cuts[0] : cuts[1]],
        grads[:, :, cuts[1] : cuts[2]],
        grads[:, :, cuts[2] : cuts[3]],
        grads[:, :, cuts[3] :],
    )
    at_in, at_one = 2, 2 + b_in.shape[1] // width
    at_two = at_one + 3
    return (
        swap(encoded),
        swap(g_tokens),
        g_qkv.reshape(layers, kept, 3, col_width),
        small[:, :at_in],
        g_out.transpose(0, 2, 1),
        small[:, at_one + 2],
        g_in,
        small[:, at_in:at_one].reshape(layers, -1),
        g_down.transpose(0, 2, 1),
        small[:, at_two + 2],
        jnp.stack([small[:, at_one], small[:, at_two]], axis=1),
        jnp.stack([small[:, at_one + 1], small[:, at_two + 1]], axis=1),
    )


def solution(mesh):
    placed = (
        P(("dp", "tensor"), None),
        P("dp", None),
        P(None, "dp", None, "tensor"),
        P(),
        P(None, "tensor", "dp"),
        P(),
        P(None, "dp", "tensor"),
        P(),
        P(None, "tensor", "dp"),
        P(),
        P(),
        P(),
        P(("dp", "tensor"), None),
    )
    return jax.shard_map(
        shards,
        mesh=mesh,
        in_specs=placed,
        out_specs=(
            P(("dp", "tensor"), None),
            P(("dp", "tensor"), None),
            P(None, "dp", None, "tensor"),
            P(),
            P(None, "tensor", "dp"),
            P(),
            P(None, "dp", "tensor"),
            P(),
            P(None, "tensor", "dp"),
            P(),
            P(),
            P(),
        ),
        check_vma=False,
    )
```

time: 1560 us -> 661 us (0.42)
  waiting for transfers between devices: 1250 us -> 164 us
  Pallas kernels: 0 us -> 309 us
  blocking collectives: 82.3 us -> 0 us
  starting transfers between devices: 2.08 us -> 37.3 us
  other arithmetic: 48.2 us -> 18.8 us
  matrix products: 109 us -> 81.3 us
    reduce_scatter x9 -> x1, waiting for transfers between devices: 603 us -> 90.8 us  [shards(): lax.psum_scatter(weight_grads, AXES, scatter_dimension=0, axis_index_grou...]
    all_gather x12 -> x1, waiting for transfers between devices: 375 us -> 0.02 us  [shards(): lax.all_gather(later_weights, AXES, axis_index_groups=PLANES, axis=0, til...]
    pallas_call x0 -> x9, Pallas kernels: none -> 309 us  [the longest x7 189 us: group_call(): pl.pallas_call(kernel, out_shape=shapes, in_specs=[VMEM] * len(operands),...]
    unnamed x24 -> x3, waiting for transfers between devices: 132 us -> 0.05 us
    all_gather x4 -> x0, blocking collectives: 82.3 us -> none  [the longest x2 48.2 us: shards(): lax.all_gather(w_qkv[layer_at], 'dp', axis=0, tiled=True)]
    psum x1, waiting for transfers between devices: 143 us -> 72.7 us  [shards(): small = lax.psum(jnp.stack(small_list), AXES)]
    ppermute x0 -> x8, starting transfers between devices: none -> 37.2 us  [swap(): return lax.ppermute(values, AXES, SWAP)]
    dot_general x22 -> x24, matrix products: 71.8 us -> 52 us  [the longest x2 14.4 us: shards(): pre_gelu = jnp.dot(mlp_input, full_in, preferred_element_type=F32) + bias_in]
  transfers between devices with their start and end apart: 23 -> 11, of which waited for: 21 -> 3; matrix products, arithmetic and copies ran while one was open for 6% -> 9% of each run, Pallas kernels for 0% -> 31%
where the time goes in v1:
time: 661 us; the launch traced here: 652 us
  Pallas kernels  309 us (47%)
  waiting for transfers between devices  164 us (25%)
  matrix products  81.3 us (12%)
  starting transfers between devices  37.3 us (6%)
  local copies, waits for them, and re-layouts  25.8 us (4%)
  other arithmetic  18.8 us (3%)
  between operations  15.1 us (2%)
    pallas_call x7, Pallas kernels, group_call(): pl.pallas_call(kernel, out_shape=shapes, in_specs=[VMEM] * len(operands),...  189 us
    reduce_scatter x1, waiting for transfers between devices, shards(): lax.psum_scatter(weight_grads, AXES, scatter_dimension=0, axis_index_grou...  90.8 us
    psum x1, waiting for transfers between devices, shards(): small = lax.psum(jnp.stack(small_list), AXES)  72.7 us
    pallas_call x1, Pallas kernels, end(): pl.pallas_call(end_kernel, out_shape=(jax.ShapeDtypeStruct((rows, width),...  61.1 us
    pallas_call x1, Pallas kernels, start(): pl.pallas_call(start_kernel, out_shape=(jax.ShapeDtypeStruct((8, rows, wi...  59 us
    ppermute x8, starting transfers between devices, swap(): return lax.ppermute(values, AXES, SWAP)  37.2 us
    dot_general x2, matrix products, shards(): pre_gelu = jnp.dot(mlp_input, full_in, preferred_element_type=F32) + bias_in  14.4 us
  transfers between devices with their start and end apart: 11, of which 3 were waited for; matrix products, arithmetic and copies ran while one was open for 9% of the time, Pallas kernels for 31%

profile of v1, /device:TPU:1, one launch (start us, length us, event | category | flops | bytes accessed | tf_op | source)
XLA Modules:
  0.0 651.6 jit_solution(2678310690077560935)
XLA Ops:
  7.3 6.0 collective-permute-start.2
  16.8 1.9 collective-permute-start.1
  18.8 5.1 collective-permute-start.3
  23.9 1.9 collective-permute-start
  25.9 5.1 collective-permute-start.4
  33.4 59.0 %start.1 = (bf16[8,128,1024]{2,1,0:T(8,128)(2,1)S(1)}, bf16[16,64,1536]{2,1,0:T(8,128)(2,1)S(1)}) custom-call(bf16[128,1024]{1,0:T(8,128)(2,1)S(1)} %collective-permute-done.tokens, bf16[64,1536]{1,0:T(8,128)(2,1)S(1)} %collective-permute-done.1.weights), custom_call_target="tpu_custom_call" | custom-call | tf_op jit(solution)/shard_map/start/pallas_call | solution.py:366
  93.8 1.9 fusion.74
  96.9 1.5 fusion.35
  99.8 28.9 %forward.3 = (f32[128,1024]{1,0:T(8,128)S(1)}, f32[128,1024]{1,0:T(8,128)S(1)}, bf16[8,128,1024]{2,1,0:T(8,128)(2,1)S(1)}) custom-call(bf16[8,128,1024]{2,1,0:T(8,128)(2,1)S(1)} %bitcast.225, f32[128,1024]{1,0:T(8,128)S(1)} %convert_element_type.309.held, f32[8,1024]{1,0:T(8,128)S(1)} %stack.81.vectors), custom_call_target="tpu_custom_call" | custom-call | tf_op jit(solution)/shard_map/forward/pallas_call | solution.py:460
  128.6 7.1 %multiply_convert_fusion.3 = (bf16[1024,512]{1,0:T(8,128)(2,1)S(1)}, f32[1024,512]{1,0:T(8,128)}, f32[1024,512]{1,0:T(8,128)}) fusion(f32[512]{0:T(512)S(1)} %bitcast.288, bf16[1024,1024]{1,0:T(8,128)(2,1)S(1)} %bitcast.243, bf16[1024,1536]{1,0:T(8,128)(2,1)S(1)} %bitcast.235), kind=kOutput, calls=%fused_computation.45 | convolution fusion | flops 1108344832 | bytes 8390656 | tf_op jit(solution)/shard_map/dot_general | solution.py:674
  137.0 27.2 %forward.4 = (f32[128,1024]{1,0:T(8,128)S(1)}, f32[128,1024]{1,0:T(8,128)S(1)}, bf16[8,128,1024]{2,1,0:T(8,128)(2,1)S(1)}) custom-call(bf16[8,128,1024]{2,1,0:T(8,128)(2,1)S(1)} %bitcast.231, f32[128,1024]{1,0:T(8,128)S(1)} %get-tuple-element.41.held, f32[8,1024]{1,0:T(8,128)S(1)} %stack.82.vectors), custom_call_target="tpu_custom_call" | custom-call | tf_op jit(solution)/shard_map/forward/pallas_call | solution.py:460
  165.5 2.9 add_convert_fusion.2
  168.4 1.9 fusion.75
  171.5 1.5 fusion.34
  175.9 25.8 %forward.5 = (f32[128,1024]{1,0:T(8,128)S(1)}, f32[128,1024]{1,0:T(8,128)S(1)}, bf16[8,128,1024]{2,1,0:T(8,128)(2,1)S(1)}) custom-call(bf16[8,128,1024]{2,1,0:T(8,128)(2,1)S(1)} %bitcast.226, f32[128,1024]{1,0:T(8,128)S(1)} %get-tuple-element.43.held, f32[8,1024]{1,0:T(8,128)S(1)} %stack.83.vectors), custom_call_target="tpu_custom_call" | custom-call | tf_op jit(solution)/shard_map/forward/pallas_call | solution.py:460
  201.7 7.3 %multiply_convert_fusion.2 = (bf16[1024,512]{1,0:T(8,128)(2,1)S(1)}, f32[1024,512]{1,0:T(8,128)}, f32[1024,512]{1,0:T(8,128)}) fusion(f32[512]{0:T(512)S(1)} %bitcast.290, bf16[1024,1024]{1,0:T(8,128)(2,1)S(1)} %bitcast.249, bf16[1024,1536]{1,0:T(8,128)(2,1)S(1)} %copy-done.23), kind=kOutput, calls=%fused_computation.32 | convolution fusion | flops 1108344832 | bytes 8390656 | tf_op jit(solution)/shard_map/dot_general | solution.py:674
  210.3 27.8 %turn.1 = (bf16[128,1024]{1,0:T(8,128)(2,1)S(1)}, f32[128,1024]{1,0:T(8,128)S(1)}, f32[8,1024]{1,0:T(8,128)S(1)}, bf16[8,128,1024]{2,1,0:T(8,128)(2,1)S(1)}) custom-call(bf16[8,128,1024]{2,1,0:T(8,128)(2,1)S(1)} %bitcast.230, f32[128,1024]{1,0:T(8,128)S(1)} %get-tuple-element.45.held, f32[8,1024]{1,0:T(8,128)S(1)} %stack.84.vectors, ...), custom_call_target="tpu_custom_call" | custom-call | tf_op jit(solution)/shard_map/turn/pallas_call | solution.py:460
  238.2 3.6 convolution_convert_fusion.8
  241.8 2.0 convert_reduce_fusion
  243.8 2.3 convolution_convert_fusion.9
  247.3 25.9 %backward.3 = (f32[128,1024]{1,0:T(8,128)S(1)}, f32[8,1024]{1,0:T(8,128)S(1)}, bf16[8,128,1024]{2,1,0:T(8,128)(2,1)S(1)}) custom-call(bf16[8,128,1024]{2,1,0:T(8,128)(2,1)S(1)} %bitcast.228, f32[128,1024]{1,0:T(8,128)S(1)} %get-tuple-element.48.held, f32[8,1024]{1,0:T(8,128)S(1)} %stack.83.vectors, f32[128,1024]{1,0:T(8,128)S(1)} %get-tuple-element.49.stream), custom_call_target="tpu_custom_call" | custom-call | tf_op jit(solution)/shard_map/backward/pallas_call | solution.py:460
  273.2 1.5 convolution_convert_fusion.15
  275.6 4.9 fusion.27
  280.5 1.9 multiply_reduce_fusion.1
  282.4 2.7 multiply_convert_fusion.1
  285.1 1.4 fusion.32
  288.1 2.2 convolution_convert_fusion.13
  291.6 28.1 %backward.4 = (f32[128,1024]{1,0:T(8,128)S(1)}, f32[8,1024]{1,0:T(8,128)S(1)}, bf16[8,128,1024]{2,1,0:T(8,128)(2,1)S(1)}) custom-call(bf16[8,128,1024]{2,1,0:T(8,128)(2,1)S(1)} %bitcast.227, f32[128,1024]{1,0:T(8,128)S(1)} %get-tuple-element.51.held, f32[8,1024]{1,0:T(8,128)S(1)} %stack.82.vectors, f32[128,1024]{1,0:T(8,128)S(1)} %get-tuple-element.52.stream), custom_call_target="tpu_custom_call" | custom-call | tf_op jit(solution)/shard_map/backward/pallas_call | solution.py:460
  319.7 4.9 convert_reduce_fusion.1
  326.0 25.8 %backward.5 = (f32[128,1024]{1,0:T(8,128)S(1)}, f32[8,1024]{1,0:T(8,128)S(1)}, bf16[8,128,1024]{2,1,0:T(8,128)(2,1)S(1)}) custom-call(bf16[8,128,1024]{2,1,0:T(8,128)(2,1)S(1)} %bitcast.229, f32[128,1024]{1,0:T(8,128)S(1)} %get-tuple-element.54.held, f32[8,1024]{1,0:T(8,128)S(1)} %stack.81.vectors, f32[128,1024]{1,0:T(8,128)S(1)} %get-tuple-element.55.stream), custom_call_target="tpu_custom_call" | custom-call | tf_op jit(solution)/shard_map/backward/pallas_call | solution.py:460
  352.6 4.9 fusion.24
  357.6 4.8 multiply_reduce_fusion
  362.4 2.5 multiply_convert_fusion
  364.9 2.1 fusion.30
  367.0 1.5 fusion.31
  369.2 2.0 convert_reduce_fusion.3
  372.3 3.1 pad_maximum_fusion.1
  376.3 1.9 collective-permute-start.5
  378.7 2.3 convolution_convert_fusion.12
  384.2 1.9 pad_maximum_fusion
  386.1 4.7 copy.67
  390.8 2.4 convolution_convert_fusion
  393.2 61.1 %end.1 = (bf16[128,1024]{1,0:T(8,128)(2,1)S(1)}, f32[64,1536]{1,0:T(8,128)S(1)}) custom-call(bf16[8,128,1024]{2,1,0:T(8,128)(2,1)S(1)} %bitcast.232, f32[128,1024]{1,0:T(8,128)S(1)} %get-tuple-element.57.held, bf16[16,64,1536]{2,1,0:T(8,128)(2,1)} %bitcast.257), custom_call_target="tpu_custom_call" | custom-call | tf_op jit(solution)/shard_map/end/pallas_call | solution.py:491
  454.4 4.9 collective-permute-start.6
  459.3 72.7 %all-reduce.2.cloned.1.call-done = f32[2,12,1024]{2,1,0:T(8,128)} async-done(((f32[2,12,1024]{2,1,0:T(8,128)}), f32[2,12,1024]{2,1,0:T(8,128)}) %all-reduce.2.cloned.1.call-update) | async-done | bytes 98320 | tf_op jit(solution)/shard_map/psum | solution.py:789
  533.1 90.8 %reduce-scatter.2.cloned.1.call-done = bf16[64,1536]{1,0:T(8,128)(2,1)} async-done(((bf16[1024,1536]{1,0:T(8,128)(2,1)}), bf16[64,1536]{1,0:T(8,128)(2,1)}) %reduce-scatter.2.cloned.1.call-update) | async-done | bytes 196624 | tf_op jit(solution)/shard_map/reduce_scatter | solution.py:776
  624.9 10.2 %collective-permute-start.7 = (bf16[2,64,1536]{2,1,0:T(8,128)(2,1)S(1)}, bf16[2,64,1536]{2,1,0:T(8,128)(2,1)S(1)}, u32[]{:S(2)}, u32[]{:S(2)}) collective-permute-start(bf16[2,64,1536]{2,1,0:T(8,128)(2,1)S(1)} %pad_maximum_fusion.2), channel_id=1, source_target_pairs={{0,0},{8,4},{16,16},{24,20},{32,32},{40,36},{48,48},{56,52},{1,1},... | collective-permute-start | bytes 1179656 | tf_op jit(solution)/shard_map/ppermute | solution.py:581
  637.8 1.4 slice.305
  (190 shorter events, 41.1 us)
Async XLA Ops:
  7.2 23.9 %copy-start.29 = (bf16[2,2,1024]{2,1,0:T(2,128)(2,1)S(1)}, bf16[2,2,1024]{2,1,0:T(2,128)(2,1)}, u32[]{:S(2)}) copy-start(bf16[2,2,1024]{2,1,0:T(2,128)(2,1)} %param.16) | copy-start | bytes 24580
  7.2 23.9 %copy-start.27 = (bf16[2,1024]{1,0:T(2,128)(2,1)S(1)}, bf16[2,1024]{1,0:T(2,128)(2,1)}, u32[]{:S(2)}) copy-start(bf16[2,1024]{1,0:T(2,128)(2,1)} %param.18) | copy-start | bytes 12292
  7.2 23.9 %copy-start.28 = (bf16[2,1024]{1,0:T(2,128)(2,1)S(1)}, bf16[2,1024]{1,0:T(2,128)(2,1)}, u32[]{:S(2)}) copy-start(bf16[2,1024]{1,0:T(2,128)(2,1)} %param.22) | copy-start | bytes 12292
  7.2 23.9 %copy-start.24 = (bf16[2,4096]{1,0:T(2,128)(2,1)S(1)}, bf16[2,4096]{1,0:T(2,128)(2,1)}, u32[]{:S(2)}) copy-start(bf16[2,4096]{1,0:T(2,128)(2,1)} %param.20) | copy-start | bytes 49156
  7.2 24.0 %copy-start.25 = (bf16[2,2,1024]{2,1,0:T(2,128)(2,1)S(1)}, bf16[2,2,1024]{2,1,0:T(2,128)(2,1)}, u32[]{:S(2)}) copy-start(bf16[2,2,1024]{2,1,0:T(2,128)(2,1)} %param.24) | copy-start | bytes 24580
  7.2 24.0 %copy-start.26 = (bf16[2,2,1024]{2,1,0:T(2,128)(2,1)S(1)}, bf16[2,2,1024]{2,1,0:T(2,128)(2,1)}, u32[]{:S(2)}) copy-start(bf16[2,2,1024]{2,1,0:T(2,128)(2,1)} %param.23) | copy-start | bytes 24580
  7.2 158.3 %all-gather.2.cloned.1.call-start = ((), (), s32[]{:S(2)}) async-start(), calls=%async_computation.1 | async-start | bytes 3342336 | tf_op jit(solution)/shard_map/all_gather | solution.py:628
  7.3 25.0 %collective-permute-start.2 = (s32[1,4]{1,0:T(1,128)}, s32[1,4]{1,0:T(1,128)S(1)}, u32[]{:S(2)}, u32[]{:S(2)}) collective-permute-start(s32[1,4]{1,0:T(1,128)} %param.14), channel_id=1, source_target_pairs={{0,0},{8,4},{16,16},{24,20},{32,32},{40,36},{48,48},{56,52},{1,1},... | collective-permute-start | bytes 56 | tf_op jit(solution)/shard_map/ppermute | solution.py:581
  16.8 16.6 %collective-permute-start.1 = (bf16[64,1536]{1,0:T(8,128)(2,1)S(1)}, bf16[64,1536]{1,0:T(8,128)(2,1)S(1)}, u32[]{:S(2)}, u32[]{:S(2)}) collective-permute-start(bf16[64,1536]{1,0:T(8,128)(2,1)S(1)} %pad_maximum_fusion.3), channel_id=1, source_target_pairs={{0,0},{8,4},{16,16},{24,20},{32,32},{40,36},{48,48},{56,52},{1,1},... | collective-permute-start | bytes 589832 | tf_op jit(solution)/shard_map/ppermute | solution.py:581
  18.8 12.7 %collective-permute-start.3 = (bf16[64,1536]{1,0:T(8,128)(2,1)S(1)}, bf16[64,1536]{1,0:T(8,128)(2,1)S(1)}, u32[]{:S(2)}, u32[]{:S(2)}) collective-permute-start(bf16[64,1536]{1,0:T(8,128)(2,1)S(1)} %pad_maximum_fusion.4), channel_id=1, source_target_pairs={{0,0},{8,4},{16,16},{24,20},{32,32},{40,36},{48,48},{56,52},{1,1},... | collective-permute-start | bytes 589832 | tf_op jit(solution)/shard_map/ppermute | solution.py:581
  23.9 9.4 %collective-permute-start = (bf16[128,1024]{1,0:T(8,128)(2,1)}, bf16[128,1024]{1,0:T(8,128)(2,1)S(1)}, u32[]{:S(2)}, u32[]{:S(2)}) collective-permute-start(bf16[128,1024]{1,0:T(8,128)(2,1)} %param.13), channel_id=1, source_target_pairs={{0,0},{8,4},{16,16},{24,20},{32,32},{40,36},{48,48},{56,52},{1,1},... | collective-permute-start | bytes 786440 | tf_op jit(solution)/shard_map/ppermute | solution.py:581
  25.9 184.4 %collective-permute-start.4 = (bf16[128,1024]{1,0:T(8,128)(2,1)}, bf16[128,1024]{1,0:T(8,128)(2,1)S(1)}, u32[]{:S(2)}, u32[]{:S(2)}) collective-permute-start(bf16[128,1024]{1,0:T(8,128)(2,1)} %param.25), channel_id=1, source_target_pairs={{0,0},{8,4},{16,16},{24,20},{32,32},{40,36},{48,48},{56,52},{1,1},... | collective-permute-start | bytes 786440 | tf_op jit(solution)/shard_map/ppermute | solution.py:581
  32.2 499.8 %all-reduce.2.cloned.1.call-start = ((), (), s32[]{:S(2)}) async-start(), calls=%async_computation.3 | async-start | bytes 262144 | tf_op jit(solution)/shard_map/psum | solution.py:789
  33.3 60.5 %copy-start.19 = (pred[1024,1024]{0,1:T(8,128)(4,1)}, pred[1024,1024]{0,1:T(8,128)(4,1)S(1)}, u32[]{:S(2)}) copy-start(pred[1024,1024]{0,1:T(8,128)(4,1)S(1)} %broadcast_compare_fusion) | copy-start | bytes 3145732
  92.4 1.4 copy-start.2
  92.4 43.3 %copy-start = (bf16[16,64,1536]{2,1,0:T(8,128)(2,1)}, bf16[16,64,1536]{2,1,0:T(8,128)(2,1)S(1)}, u32[]{:S(2)}) copy-start(bf16[16,64,1536]{2,1,0:T(8,128)(2,1)S(1)} %get-tuple-element.39) | copy-start | bytes 9437188
  93.8 3.1 copy-start.15
  95.7 3.3 copy-start.12
  99.0 29.6 %copy-start.17 = (bf16[2,64,1024]{2,1,0:T(8,128)(2,1)}, bf16[2,64,1024]{2,1,0:T(8,128)(2,1)S(1)}, u32[]{:S(2)}) copy-start(bf16[2,64,1024]{2,1,0:T(8,128)(2,1)S(1)} %fusion.35) | copy-start | bytes 786436
  128.6 7.1 %copy-start.4 = (bf16[8,128,1024]{2,1,0:T(8,128)(2,1)}, bf16[8,128,1024]{2,1,0:T(8,128)(2,1)S(1)}, u32[]{:S(2)}) copy-start(bf16[8,128,1024]{2,1,0:T(8,128)(2,1)S(1)} %get-tuple-element.40) | copy-start | bytes 6291460
  164.2 1.3 copy-start.8
  165.5 2.9 copy-start.20
  170.4 3.7 copy-start.13
  171.5 3.7 copy-start.23
  238.1 3.7 copy-start.10
  238.1 3.7 copy-start.35
  238.2 3.7 copy-start.36
  273.2 7.3 %slice-start.2 = ((s8[8388608]{0:T(1024)(128)(4,1)}), s8[4194304]{0:T(1024)(128)(4,1)S(1)}, s32[]{:S(2)}) async-start(s8[8388608]{0:T(1024)(128)(4,1)} %bitcast.255), calls=%async_computation.6 | async-start | bytes 8388608
  275.6 5.0 slice-start.3
  286.5 1.6 copy-start.9
  291.6 28.1 %copy-start.1 = (bf16[16,64,1536]{2,1,0:T(8,128)(2,1)S(1)}, bf16[16,64,1536]{2,1,0:T(8,128)(2,1)}, u32[]{:S(2)}) copy-start(bf16[16,64,1536]{2,1,0:T(8,128)(2,1)} %copy-done) | copy-start | bytes 9437188
  319.7 4.9 copy-start.6
  324.7 1.3 copy-start.32
  352.6 5.0 copy-start.16
  352.6 9.7 %slice-start = ((s8[8388608]{0:T(1024)(128)(4,1)}), s8[4194304]{0:T(1024)(128)(4,1)S(1)}, s32[]{:S(2)}) async-start(s8[8388608]{0:T(1024)(128)(4,1)} %bitcast.253), calls=%async_computation.4 | async-start | bytes 8388608
  357.6 4.8 slice-start.1
  368.5 3.7 copy-start.14
  372.2 251.7 %reduce-scatter.2.cloned.1.call-start = ((), (), s32[]{:S(2)}) async-start(), calls=%async_computation.2 | async-start | bytes 3342336 | tf_op jit(solution)/shard_map/reduce_scatter | solution.py:776
  375.3 2.9 copy-start.18
  375.4 3.3 copy-start.3
  376.3 264.2 %collective-permute-start.5 = (bf16[128,1024]{1,0:T(8,128)(2,1)S(1)}, bf16[128,1024]{1,0:T(8,128)(2,1)S(1)}, u32[]{:S(2)}, u32[]{:S(2)}) collective-permute-start(bf16[128,1024]{1,0:T(8,128)(2,1)S(1)} %copy-done.11), channel_id=1, source_target_pairs={{0,0},{8,4},{16,16},{24,20},{32,32},{40,36},{48,48},{56,52},{1,1},... | collective-permute-start | bytes 786440 | tf_op jit(solution)/shard_map/ppermute | solution.py:581
  378.7 2.3 copy-start.7
  378.7 2.3 copy-start.31
  381.0 1.6 copy-start.5
  381.0 1.8 copy-start.33
  386.1 4.7 copy-start.21
  454.4 186.1 %collective-permute-start.6 = (bf16[128,1024]{1,0:T(8,128)(2,1)S(1)}, bf16[128,1024]{1,0:T(8,128)(2,1)S(1)}, u32[]{:S(2)}, u32[]{:S(2)}) collective-permute-start(bf16[128,1024]{1,0:T(8,128)(2,1)S(1)} %get-tuple-element.58), channel_id=1, source_target_pairs={{0,0},{8,4},{16,16},{24,20},{32,32},{40,36},{48,48},{56,52},{1,1},... | collective-permute-start | bytes 786440 | tf_op jit(solution)/shard_map/ppermute | solution.py:581
  624.9 15.7 %collective-permute-start.7 = (bf16[2,64,1536]{2,1,0:T(8,128)(2,1)S(1)}, bf16[2,64,1536]{2,1,0:T(8,128)(2,1)S(1)}, u32[]{:S(2)}, u32[]{:S(2)}) collective-permute-start(bf16[2,64,1536]{2,1,0:T(8,128)(2,1)S(1)} %pad_maximum_fusion.2), channel_id=1, source_target_pairs={{0,0},{8,4},{16,16},{24,20},{32,32},{40,36},{48,48},{56,52},{1,1},... | collective-permute-start | bytes 1179656 | tf_op jit(solution)/shard_map/ppermute | solution.py:581
  (4 other events, 4.2 us)
Sparse Core Ops, SparseCore 0:
  32.3 96.3 all-gather.1
  372.3 159.6 all-reduce.1
  534.6 89.2 reduce-scatter.1
